TPU v7x, 32 devices: a whole 2x2x4 slice. The times are simulated.
32 devices in a mesh: ch: 16 (over z, y, core), freq: 2 (over x).
Axes of the slice: x: 2, y: 2, z: 4, core: 2. Of those that a mesh axis runs over, the one named last changes fastest.
Arguments:
- strain: bfloat16 [512, 8, 2048], P('ch'), may hold values from -100 to 100
- channel_ok: int32 [512], P('ch'), may hold values 0 or 1
- window_ok: int32 [512, 8], P('ch'), may hold values 0 or 1
Outputs:
- stack_ahead: bfloat16 [2, 256, 512, 128], P(None, 'freq', 'ch')
- stack_behind: bfloat16 [2, 256, 512, 128], P(None, 'freq', 'ch')
All inputs are finite; a program needn't handle non-finite values. No bound on the sum of `channel_ok` or of `window_ok` on one device may be relied on, other than what follows from the above.
Results may differ from a plain program's by a relative error of at most 0.0082.
Values may be sent and summed in bfloat16 or wider, within the bound.
No kernel may reach another device: no remote copies, remote signals or barrier semaphores. Data moves between devices by JAX's collectives and lax.ppermute only.
A program may use at most 64 MiB of HBM per device.

v0:
```python
import math

import jax
import jax.numpy as jnp
from jax import lax
from jax.sharding import PartitionSpec as P

WINDOWS = 8
SAMPLES = 2048
BINS = 256
REACH = 128
TIME_HALF = 128
BIN_HALF = 32
AHEAD = 4


def extended(block, sides, width):
    for axis, dim in sides:
        count = lax.axis_size(axis)
        forward = [(i, i + 1) for i in range(count - 1)]
        backward = [(target, source) for source, target in forward]
        low = lax.ppermute(
            lax.slice_in_dim(block, block.shape[dim] - width, None, axis=dim), axis, forward
        )
        high = lax.ppermute(lax.slice_in_dim(block, 0, width, axis=dim), axis, backward)
        block = jnp.concatenate([low, block, high], axis=dim)
    return block


def from_behind(value, axis, by):
    peers = lax.axis_size(axis)
    pairs = [(i, i + by) for i in range(peers) if 0 <= i + by < peers]
    return lax.ppermute(value, axis, pairs)


def skew_take(dense_mat, offset, reach_cols):
    leading = dense_mat.shape[:-2]
    row_count = dense_mat.shape[-2]
    col_count = dense_mat.shape[-1]
    flattened = dense_mat.reshape(leading + (row_count * col_count,))[..., offset:]
    widths = [(0, 0)] * len(leading) + [(0, row_count + offset)]
    flattened = jnp.pad(flattened, widths)
    return flattened.reshape(leading + (row_count, col_count + 1))[..., :reach_cols]


def dft_table(first_bin, bin_count):
    bin_freq = first_bin + 1 + lax.iota(jnp.int32, bin_count)
    sample_ids = lax.iota(jnp.int32, SAMPLES)
    phase = (bin_freq[:, None] * sample_ids[None, :] % SAMPLES).astype(jnp.float32) * (
        2.0 * math.pi / SAMPLES
    )
    norm_scale = 1.0 / math.sqrt(SAMPLES)
    return jnp.stack([jnp.cos(phase) * norm_scale, -jnp.sin(phase) * norm_scale], axis=1).astype(
        jnp.bfloat16
    )


def level_windows(samples_in):
    channels, count, length = samples_in.shape
    block = 2 * TIME_HALF
    piece_count = length // block
    magnitude = jnp.abs(samples_in).reshape(channels, count, piece_count, block)
    zero_block = jnp.zeros_like(magnitude[:, :, :1])
    previous = jnp.concatenate([zero_block, magnitude[:, :, :-1]], axis=2)
    following = jnp.concatenate([magnitude[:, :, 1:], zero_block], axis=2)
    widened = jnp.concatenate([previous, magnitude, following], axis=3)
    source_ids = lax.iota(jnp.int32, 3 * block)[:, None] - block
    target_ids = lax.iota(jnp.int32, block)[None, :]
    window_ones = (jnp.abs(source_ids - target_ids) <= TIME_HALF).astype(jnp.bfloat16)
    window_sums = jnp.einsum(
        "cwnp,pq->cwnq", widened, window_ones, preferred_element_type=jnp.float32
    )
    level_mean = window_sums.reshape(channels, count, length) / (2 * TIME_HALF + 1)
    return (samples_in.astype(jnp.float32) / (level_mean + 1e-06)).astype(jnp.bfloat16)


def cross_terms(white_flat, usable_b, partners, partner_usable):
    bin_count = white_flat.shape[0]
    channels = usable_b.shape[0]
    left_rows = white_flat.reshape(bin_count, channels, 2 * WINDOWS)
    sign_flip = jnp.concatenate(
        [jnp.ones((WINDOWS,), jnp.bfloat16), -jnp.ones((WINDOWS,), jnp.bfloat16)]
    )
    left_conj = left_rows * sign_flip
    joined = jnp.concatenate(partners, axis=1).reshape(bin_count, -1, 2, WINDOWS)
    right_same = joined.reshape(bin_count, -1, 2 * WINDOWS)
    right_swap = jnp.flip(joined, axis=2).reshape(bin_count, -1, 2 * WINDOWS)
    real_part = jnp.einsum(
        "kiv,kjv->kij", left_rows, right_same, preferred_element_type=jnp.float32
    )
    imag_part = jnp.einsum(
        "kiv,kjv->kij", left_conj, right_swap, preferred_element_type=jnp.float32
    )
    counts = jnp.dot(
        usable_b, jnp.concatenate(partner_usable, axis=0).T, preferred_element_type=jnp.float32
    )
    return (real_part, imag_part, counts)


def stacks_from(real_part, imag_part, counts, offset, reverse):
    divisor = jnp.maximum(skew_take(counts, offset, REACH), 1.0)
    stacked = jnp.stack(
        [
            skew_take(real_part, offset, REACH) / divisor,
            skew_take(imag_part, offset, REACH) / divisor,
        ]
    )
    if reverse:
        stacked = jnp.flip(stacked, axis=3)
    return stacked.astype(jnp.bfloat16)


def per_device(strain, channel_ok, window_ok):
    channels = strain.shape[0]
    freq_devices = lax.axis_size("freq")
    bin_count = BINS // freq_devices
    freq_index = lax.axis_index("freq")
    spectra = jnp.einsum(
        "kps,cws->kcpw",
        dft_table(freq_index * bin_count, bin_count),
        level_windows(strain),
        preferred_element_type=jnp.float32,
    )
    band_power = spectra[:, :, 0] * spectra[:, :, 0] + spectra[:, :, 1] * spectra[:, :, 1]
    band_power = band_power.reshape(bin_count, channels * WINDOWS)
    padded = extended(band_power.astype(jnp.bfloat16), (("freq", 0),), BIN_HALF).astype(
        band_power.dtype
    )
    row_ids = lax.iota(jnp.int32, bin_count)[:, None] + BIN_HALF
    col_ids = lax.iota(jnp.int32, bin_count + 2 * BIN_HALF)[None, :]
    smoother_ones = (jnp.abs(col_ids - row_ids) <= BIN_HALF).astype(jnp.float32)
    smooth = jnp.dot(
        smoother_ones, padded, precision=lax.Precision.HIGHEST, preferred_element_type=jnp.float32
    ) / (2 * BIN_HALF + 1)
    inverse = (1.0 / jnp.sqrt(smooth + 1e-06)).reshape(bin_count, channels, 1, WINDOWS)
    usable = (channel_ok[:, None] * window_ok).astype(jnp.float32)
    white = (spectra * inverse * usable[None, :, None, :]).astype(jnp.bfloat16)
    white_flat = white.reshape(bin_count, channels * 2 * WINDOWS)
    usable_b = usable.astype(jnp.bfloat16)
    ahead_flat = [white_flat]
    ahead_usable = [usable_b]
    for distance in range(1, AHEAD + 1):
        arrived = from_behind((white_flat, usable_b), "ch", -distance)
        ahead_flat.append(arrived[0])
        ahead_usable.append(arrived[1])
    real_part, imag_part, counts = cross_terms(white_flat, usable_b, ahead_flat, ahead_usable)
    stack_ahead = stacks_from(real_part, imag_part, counts, 1, False)
    behind_offset = AHEAD * channels - REACH
    behind_flat = []
    behind_usable = []
    for distance in range(AHEAD, 0, -1):
        arrived = from_behind((white_flat, usable_b), "ch", distance)
        behind_flat.append(arrived[0])
        behind_usable.append(arrived[1])
    behind_flat.append(white_flat)
    behind_usable.append(usable_b)
    real_back, imag_back, counts_back = cross_terms(
        white_flat, usable_b, behind_flat, behind_usable
    )
    stack_behind = stacks_from(real_back, imag_back, counts_back, behind_offset, True)
    return (stack_ahead, stack_behind)


def solution(mesh):
    placed = (P("ch", None, None), P("ch"), P("ch", None))
    return jax.shard_map(
        per_device,
        mesh=mesh,
        in_specs=placed,
        out_specs=(P(None, "freq", "ch", None), P(None, "freq", "ch", None)),
        check_vma=False,
    )
```

profile of v0, /device:TPU:25, one launch (start us, length us, event | category | flops | bytes accessed | tf_op | source)
XLA Modules:
  0.0 172.2 jit_solution(10398654765977167186)
XLA Ops:
  3.9 3.1 %collective-permute-start.16 = (bf16[32,8]{0,1:T(8,128)(2,1)S(1)}, bf16[32,8]{0,1:T(8,128)(2,1)S(1)}, u32[]{:S(2)}, u32[]{:S(2)}) collective-permute-start(bf16[32,8]{0,1:T(8,128)(2,1)S(1)} %get-tuple-element.6), channel_id=1, source_target_pairs={{0,4},{2,6},{4,8},{6,10},{8,12},{10,14},{12,16},{14,18},{16,20},{1... | collective-permute-start | bytes 1544 | tf_op jit(solution)/shard_map/ppermute | solution.py:33
  7.1 1.9 %collective-permute-start.17 = (bf16[32,8]{0,1:T(8,128)(2,1)S(1)}, bf16[32,8]{0,1:T(8,128)(2,1)S(1)}, u32[]{:S(2)}, u32[]{:S(2)}) collective-permute-start(bf16[32,8]{0,1:T(8,128)(2,1)S(1)} %get-tuple-element.6), channel_id=1, source_target_pairs={{0,2},{2,4},{4,6},{6,8},{8,10},{10,12},{12,14},{14,16},{16,18},{18... | collective-permute-start | bytes 1544 | tf_op jit(solution)/shard_map/ppermute | solution.py:33
  9.0 2.9 %collective-permute-start.6 = (bf16[32,8]{0,1:T(8,128)(2,1)S(1)}, bf16[32,8]{0,1:T(8,128)(2,1)S(1)}, u32[]{:S(2)}, u32[]{:S(2)}) collective-permute-start(bf16[32,8]{0,1:T(8,128)(2,1)S(1)} %get-tuple-element.6), channel_id=1, source_target_pairs={{2,0},{4,2},{6,4},{8,6},{10,8},{12,10},{14,12},{16,14},{18,16},{20... | collective-permute-start | bytes 1544 | tf_op jit(solution)/shard_map/ppermute | solution.py:33
  14.2 2.5 %multiply_add_fusion = f32[32,8,8,256]{3,2,1,0:T(8,128)} fusion(bf16[32,8,7,256]{3,2,1,0:T(8,128)(2,1)S(1)} %get-tuple-element.9, bf16[32,8,7,256]{3,2,1,0:T(8,128)(2,1)S(1)} %get-tuple-element.8, bf16[32,8,8,256]{3,2,1,0:T(8,128)(2,1)S(1)} %copy.41, s32[768]{0:T(1024)S(1)} %iota_add_fusion), kind=kOutput, calls=%fused_computation.23 | convolution fusion | flops 822673408 | bytes 4983808 | tf_op jit(solution)/shard_map/cwnp,pq->cwnq/dot_general | solution.py:70
  18.5 4.9 %multiply_convert_fusion.1 = (bf16[128,1,2048]{2,0,1:T(8,128)(2,1)S(1)}, bf16[128,1,2048]{2,0,1:T(8,128)(2,1)S(1)}) fusion(s32[128]{0:T(128)S(1)} %iota_add_fusion.2), kind=kLoop, calls=%fused_computation.41 | loop fusion | flops 4980736 | bytes 1049088 | tf_op jit(solution)/shard_map/convert.4
  24.2 4.5 %collective-permute-start.7 = (bf16[32,8]{0,1:T(8,128)(2,1)S(1)}, bf16[32,8]{0,1:T(8,128)(2,1)S(1)}, u32[]{:S(2)}, u32[]{:S(2)}) collective-permute-start(bf16[32,8]{0,1:T(8,128)(2,1)S(1)} %get-tuple-element.6), channel_id=1, source_target_pairs={{4,0},{6,2},{8,4},{10,6},{12,8},{14,10},{16,12},{18,14},{20,16},{2... | collective-permute-start | bytes 1544 | tf_op jit(solution)/shard_map/ppermute | solution.py:33
  28.7 6.2 %collective-permute-start.8 = (bf16[32,8]{0,1:T(8,128)(2,1)S(1)}, bf16[32,8]{0,1:T(8,128)(2,1)S(1)}, u32[]{:S(2)}, u32[]{:S(2)}) collective-permute-start(bf16[32,8]{0,1:T(8,128)(2,1)S(1)} %get-tuple-element.6), channel_id=1, source_target_pairs={{6,0},{8,2},{10,4},{12,6},{14,8},{16,10},{18,12},{20,14},{22,16},{... | collective-permute-start | bytes 1544 | tf_op jit(solution)/shard_map/ppermute | solution.py:33
  34.9 2.8 %collective-permute-start.9 = (bf16[32,8]{0,1:T(8,128)(2,1)S(1)}, bf16[32,8]{0,1:T(8,128)(2,1)S(1)}, u32[]{:S(2)}, u32[]{:S(2)}) collective-permute-start(bf16[32,8]{0,1:T(8,128)(2,1)S(1)} %get-tuple-element.6), channel_id=1, source_target_pairs={{8,0},{10,2},{12,4},{14,6},{16,8},{18,10},{20,12},{22,14},{24,16},... | collective-permute-start | bytes 1544 | tf_op jit(solution)/shard_map/ppermute | solution.py:33
  37.7 3.1 %collective-permute-start = (bf16[32,256]{0,1:T(8,128)(2,1)S(1)}, bf16[32,256]{0,1:T(8,128)(2,1)S(1)}, u32[]{:S(2)}, u32[]{:S(2)}) collective-permute-start(bf16[32,256]{0,1:T(8,128)(2,1)S(1)} %get-tuple-element.10), channel_id=1, source_target_pairs={{0,1},{2,3},{4,5},{6,7},{8,9},{10,11},{12,13},{14,15},{16,17},{18,... | collective-permute-start | bytes 49160 | tf_op jit(solution)/shard_map/ppermute | solution.py:22
  43.9 3.4 %collective-permute-done.1 = bf16[32,256]{0,1:T(8,128)(2,1)S(1)} collective-permute-done((bf16[32,256]{0,1:T(8,128)(2,1)S(1)}, bf16[32,256]{0,1:T(8,128)(2,1)S(1)}, u32[]{:S(2)}, u32[]{:S(2)}) %collective-permute-start.1) | collective-permute-done | bytes 16416 | tf_op jit(solution)/shard_map/ppermute | solution.py:25
  51.8 2.0 %collective-permute-start.12 = (bf16[128,512]{0,1:T(8,128)(2,1)S(1)}, bf16[128,512]{0,1:T(8,128)(2,1)S(1)}, u32[]{:S(2)}, u32[]{:S(2)}) collective-permute-start(bf16[128,512]{0,1:T(8,128)(2,1)S(1)} %bitcast.89), channel_id=1, source_target_pairs={{0,4},{2,6},{4,8},{6,10},{8,12},{10,14},{12,16},{14,18},{16,20},{1... | collective-permute-start | bytes 393224 | tf_op jit(solution)/shard_map/ppermute | solution.py:33
  55.7 2.9 %collective-permute-start.2 = (bf16[128,512]{0,1:T(8,128)(2,1)S(1)}, bf16[128,512]{0,1:T(8,128)(2,1)S(1)}, u32[]{:S(2)}, u32[]{:S(2)}) collective-permute-start(bf16[128,512]{0,1:T(8,128)(2,1)S(1)} %bitcast.91), channel_id=1, source_target_pairs={{2,0},{4,2},{6,4},{8,6},{10,8},{12,10},{14,12},{16,14},{18,16},{20... | collective-permute-start | bytes 393224 | tf_op jit(solution)/shard_map/ppermute | solution.py:33
  59.2 4.5 %collective-permute-start.3 = (bf16[128,512]{0,1:T(8,128)(2,1)S(1)}, bf16[128,512]{0,1:T(8,128)(2,1)S(1)}, u32[]{:S(2)}, u32[]{:S(2)}) collective-permute-start(bf16[128,512]{0,1:T(8,128)(2,1)S(1)} %bitcast.93), channel_id=1, source_target_pairs={{4,0},{6,2},{8,4},{10,6},{12,8},{14,10},{16,12},{18,14},{20,16},{2... | collective-permute-start | bytes 393224 | tf_op jit(solution)/shard_map/ppermute | solution.py:33
  63.8 6.8 %collective-permute-start.4 = (bf16[128,512]{0,1:T(8,128)(2,1)S(1)}, bf16[128,512]{0,1:T(8,128)(2,1)}, u32[]{:S(2)}, u32[]{:S(2)}) collective-permute-start(bf16[128,512]{0,1:T(8,128)(2,1)S(1)} %bitcast.94), channel_id=1, source_target_pairs={{6,0},{8,2},{10,4},{12,6},{14,8},{16,10},{18,12},{20,14},{22,16},{... | collective-permute-start | bytes 393224 | tf_op jit(solution)/shard_map/ppermute | solution.py:33
  70.6 3.9 %collective-permute-start.5 = (bf16[128,512]{0,1:T(8,128)(2,1)S(1)}, bf16[128,512]{0,1:T(8,128)(2,1)}, u32[]{:S(2)}, u32[]{:S(2)}) collective-permute-start(bf16[128,512]{0,1:T(8,128)(2,1)S(1)} %bitcast.95), channel_id=1, source_target_pairs={{8,0},{10,2},{12,4},{14,6},{16,8},{18,10},{20,12},{22,14},{24,16},... | collective-permute-start | bytes 393224 | tf_op jit(solution)/shard_map/ppermute | solution.py:33
  76.6 2.8 %fusion.34 = f32[128,32,160]{2,1,0:T(8,128)} fusion(bf16[128,160,16]{1,2,0:T(8,128)(2,1)S(1)} %copy.33, bf16[128,32,16]{1,2,0:T(8,128)(2,1)S(1)} %copy.21, bf16[16]{0:T(256)(128)(2,1)S(1)} %copy-done.6), kind=kOutput, calls=%fused_computation.51 | convolution fusion | flops 21037056 | bytes 3407904 | tf_op jit(solution)/shard_map/kiv,kjv->kij/dot_general | solution.py:91
  79.4 4.9 %copy.34 = f32[128,32,160]{0,2,1:T(8,128)} copy(f32[128,32,160]{2,1,0:T(8,128)} %fusion.34) | data formatting | bytes 5242880 | tf_op jit(solution)/shard_map/kiv,kjv->kij/dot_general | solution.py:91
  92.2 2.2 %copy.29 = bf16[128,32,16]{1,2,0:T(8,128)(2,1)} copy(bf16[128,32,16]{0,2,1:T(8,128)(2,1)} %bitcast.107) | data formatting | bytes 262144 | tf_op jit(solution)/shard_map/concatenate | solution.py:85
  94.4 2.6 %concatenate.83 = bf16[128,160,16]{1,2,0:T(8,128)(2,1)S(1)} concatenate(bf16[128,32,16]{1,2,0:T(8,128)(2,1)S(1)} %copy.26, bf16[128,32,16]{1,2,0:T(8,128)(2,1)S(1)} %copy.27, bf16[128,32,16]{1,2,0:T(8,128)(2,1)S(1)} %copy.28, bf16[128,32,16]{1,2,0:T(8,128)(2,1)} %copy.29, bf16[128,32,16]{1,2,0:T(8,128)(2,1)S(1)} %copy.21), dimensions={1} | concatenate | bytes 1310720 | tf_op jit(solution)/shard_map/concatenate | solution.py:85
  97.0 2.7 %fusion.63 = f32[128,32,160]{2,1,0:T(8,128)} fusion(bf16[128,32,16]{1,2,0:T(8,128)(2,1)S(1)} %copy.21, bf16[128,160,16]{1,2,0:T(8,128)(2,1)S(1)} %concatenate.83), kind=kOutput, calls=%fused_computation.102 | convolution fusion | flops 20971520 | bytes 3407872 | tf_op jit(solution)/shard_map/kiv,kjv->kij/dot_general | solution.py:88
  99.8 4.9 %copy.32 = f32[128,32,160]{0,2,1:T(8,128)} copy(f32[128,32,160]{2,1,0:T(8,128)} %fusion.63) | data formatting | bytes 5242880 | tf_op jit(solution)/shard_map/kiv,kjv->kij/dot_general | solution.py:88
  108.2 2.6 %fusion.13 = (bf16[1,128,32,128]{1,3,2,0:T(8,128)(2,1)S(1)}, bf16[1,128,32,128]{1,3,2,0:T(8,128)(2,1)S(1)}) fusion(f32[128,32,161]{0,2,1:T(8,128)} %reshape.224, f32[32,128]{1,0:T(8,128)} %slice_maximum_fusion, f32[128,32,161]{0,2,1:T(8,128)} %reshape.229), kind=kLoop, calls=%fused_computation.16 | loop fusion | flops 2097152 | bytes 6307840 | tf_op jit(solution)/shard_map/stack | solution.py:102
  112.4 20.2 %rev.13 = bf16[2,128,32,128]{1,3,2,0:T(8,128)(2,1)} reverse(bf16[2,128,32,128]{1,3,2,0:T(8,128)(2,1)S(1)} %pad_maximum_fusion), dimensions={3} | reverse | bytes 4194304 | tf_op jit(solution)/shard_map/jit(_flip)/rev | solution.py:109
  132.6 4.5 %copy.36 = bf16[2,128,32,128]{3,2,1,0:T(8,128)(2,1)} copy(bf16[2,128,32,128]{1,3,2,0:T(8,128)(2,1)} %rev.13) | data formatting | bytes 4194304
  142.5 2.8 %fusion.36 = f32[128,32,160]{2,1,0:T(8,128)} fusion(bf16[128,160,16]{1,2,0:T(8,128)(2,1)S(1)} %copy.24, bf16[128,32,16]{1,2,0:T(8,128)(2,1)S(1)} %copy.21, bf16[16]{0:T(256)(128)(2,1)S(1)} %copy-done.7), kind=kOutput, calls=%fused_computation.53 | convolution fusion | flops 21037056 | bytes 3407904 | tf_op jit(solution)/shard_map/kiv,kjv->kij/dot_general | solution.py:91
  145.3 3.6 %copy.25 = f32[128,32,160]{0,2,1:T(8,128)S(1)} copy(f32[128,32,160]{2,1,0:T(8,128)} %fusion.36) | data formatting | bytes 5242880 | tf_op jit(solution)/shard_map/kiv,kjv->kij/dot_general | solution.py:91
  153.4 2.2 %copy.20 = bf16[128,32,16]{1,2,0:T(8,128)(2,1)} copy(bf16[128,32,16]{0,2,1:T(8,128)(2,1)} %bitcast.15) | data formatting | bytes 262144 | tf_op jit(solution)/shard_map/concatenate | solution.py:85
  155.5 2.6 %concatenate.72 = bf16[128,160,16]{1,2,0:T(8,128)(2,1)S(1)} concatenate(bf16[128,32,16]{1,2,0:T(8,128)(2,1)S(1)} %copy.21, bf16[128,32,16]{1,2,0:T(8,128)(2,1)S(1)} %copy.17, bf16[128,32,16]{1,2,0:T(8,128)(2,1)S(1)} %copy.18, bf16[128,32,16]{1,2,0:T(8,128)(2,1)S(1)} %copy.19, bf16[128,32,16]{1,2,0:T(8,128)(2,1)} %copy.20), dimensions={1} | concatenate | bytes 1310720 | tf_op jit(solution)/shard_map/concatenate | solution.py:85
  158.2 2.7 %fusion.61 = f32[128,32,160]{2,1,0:T(8,128)} fusion(bf16[128,32,16]{1,2,0:T(8,128)(2,1)S(1)} %copy.21, bf16[128,160,16]{1,2,0:T(8,128)(2,1)S(1)} %concatenate.72), kind=kOutput, calls=%fused_computation.100 | convolution fusion | flops 20971520 | bytes 3407872 | tf_op jit(solution)/shard_map/kiv,kjv->kij/dot_general | solution.py:88
  160.9 3.6 %copy.22 = f32[128,32,160]{0,2,1:T(8,128)S(1)} copy(f32[128,32,160]{2,1,0:T(8,128)} %fusion.61) | data formatting | bytes 5242880 | tf_op jit(solution)/shard_map/kiv,kjv->kij/dot_general | solution.py:88
  166.5 2.6 %fusion.29 = (bf16[1,128,32,128]{1,3,2,0:T(8,128)(2,1)S(1)}, bf16[1,128,32,128]{1,3,2,0:T(8,128)(2,1)S(1)}) fusion(f32[32,128]{1,0:T(8,128)S(1)} %copy-done.5, f32[128,32,161]{0,2,1:T(8,128)} %reshape.217, f32[128,32,161]{0,2,1:T(8,128)} %reshape.222), kind=kLoop, calls=%fused_computation.44 | loop fusion | flops 2097152 | bytes 6307840 | tf_op jit(solution)/shard_map/stack | solution.py:102
  169.3 2.9 %copy.35 = bf16[2,128,32,128]{3,2,1,0:T(8,128)(2,1)} copy(bf16[2,128,32,128]{1,3,2,0:T(8,128)(2,1)S(1)} %pad_maximum_fusion.1) | data formatting | bytes 4194304
  (100 shorter events, 44.8 us)
Async XLA Ops:
  1.3 22.9 %collective-permute-start.14 = (bf16[32,8]{0,1:T(8,128)(2,1)S(1)}, bf16[32,8]{0,1:T(8,128)(2,1)S(1)}, u32[]{:S(2)}, u32[]{:S(2)}) collective-permute-start(bf16[32,8]{0,1:T(8,128)(2,1)S(1)} %get-tuple-element.6), channel_id=1, source_target_pairs={{0,8},{2,10},{4,12},{6,14},{8,16},{10,18},{12,20},{14,22},{16,24},... | collective-permute-start | bytes 1544 | tf_op jit(solution)/shard_map/ppermute | solution.py:33
  2.6 26.1 %collective-permute-start.15 = (bf16[32,8]{0,1:T(8,128)(2,1)S(1)}, bf16[32,8]{0,1:T(8,128)(2,1)S(1)}, u32[]{:S(2)}, u32[]{:S(2)}) collective-permute-start(bf16[32,8]{0,1:T(8,128)(2,1)S(1)} %get-tuple-element.6), channel_id=1, source_target_pairs={{0,6},{2,8},{4,10},{6,12},{8,14},{10,16},{12,18},{14,20},{16,22},{... | collective-permute-start | bytes 1544 | tf_op jit(solution)/shard_map/ppermute | solution.py:33
  3.9 31.0 %collective-permute-start.16 = (bf16[32,8]{0,1:T(8,128)(2,1)S(1)}, bf16[32,8]{0,1:T(8,128)(2,1)S(1)}, u32[]{:S(2)}, u32[]{:S(2)}) collective-permute-start(bf16[32,8]{0,1:T(8,128)(2,1)S(1)} %get-tuple-element.6), channel_id=1, source_target_pairs={{0,4},{2,6},{4,8},{6,10},{8,12},{10,14},{12,16},{14,18},{16,20},{1... | collective-permute-start | bytes 1544 | tf_op jit(solution)/shard_map/ppermute | solution.py:33
  7.1 30.6 %collective-permute-start.17 = (bf16[32,8]{0,1:T(8,128)(2,1)S(1)}, bf16[32,8]{0,1:T(8,128)(2,1)S(1)}, u32[]{:S(2)}, u32[]{:S(2)}) collective-permute-start(bf16[32,8]{0,1:T(8,128)(2,1)S(1)} %get-tuple-element.6), channel_id=1, source_target_pairs={{0,2},{2,4},{4,6},{6,8},{8,10},{10,12},{12,14},{14,16},{16,18},{18... | collective-permute-start | bytes 1544 | tf_op jit(solution)/shard_map/ppermute | solution.py:33
  9.0 32.3 %collective-permute-start.6 = (bf16[32,8]{0,1:T(8,128)(2,1)S(1)}, bf16[32,8]{0,1:T(8,128)(2,1)S(1)}, u32[]{:S(2)}, u32[]{:S(2)}) collective-permute-start(bf16[32,8]{0,1:T(8,128)(2,1)S(1)} %get-tuple-element.6), channel_id=1, source_target_pairs={{2,0},{4,2},{6,4},{8,6},{10,8},{12,10},{14,12},{16,14},{18,16},{20... | collective-permute-start | bytes 1544 | tf_op jit(solution)/shard_map/ppermute | solution.py:33
  16.7 6.7 %copy-start = (bf16[32,8,2048]{2,1,0:T(8,128)(2,1)S(1)}, bf16[32,8,2048]{2,1,0:T(8,128)(2,1)}, u32[]{:S(2)}) copy-start(bf16[32,8,2048]{2,1,0:T(8,128)(2,1)} %param.3) | copy-start | bytes 3145732
  24.2 18.4 %collective-permute-start.7 = (bf16[32,8]{0,1:T(8,128)(2,1)S(1)}, bf16[32,8]{0,1:T(8,128)(2,1)S(1)}, u32[]{:S(2)}, u32[]{:S(2)}) collective-permute-start(bf16[32,8]{0,1:T(8,128)(2,1)S(1)} %get-tuple-element.6), channel_id=1, source_target_pairs={{4,0},{6,2},{8,4},{10,6},{12,8},{14,10},{16,12},{18,14},{20,16},{2... | collective-permute-start | bytes 1544 | tf_op jit(solution)/shard_map/ppermute | solution.py:33
  28.7 13.9 %collective-permute-start.8 = (bf16[32,8]{0,1:T(8,128)(2,1)S(1)}, bf16[32,8]{0,1:T(8,128)(2,1)S(1)}, u32[]{:S(2)}, u32[]{:S(2)}) collective-permute-start(bf16[32,8]{0,1:T(8,128)(2,1)S(1)} %get-tuple-element.6), channel_id=1, source_target_pairs={{6,0},{8,2},{10,4},{12,6},{14,8},{16,10},{18,12},{20,14},{22,16},{... | collective-permute-start | bytes 1544 | tf_op jit(solution)/shard_map/ppermute | solution.py:33
  34.9 7.7 %collective-permute-start.9 = (bf16[32,8]{0,1:T(8,128)(2,1)S(1)}, bf16[32,8]{0,1:T(8,128)(2,1)S(1)}, u32[]{:S(2)}, u32[]{:S(2)}) collective-permute-start(bf16[32,8]{0,1:T(8,128)(2,1)S(1)} %get-tuple-element.6), channel_id=1, source_target_pairs={{8,0},{10,2},{12,4},{14,6},{16,8},{18,10},{20,12},{22,14},{24,16},... | collective-permute-start | bytes 1544 | tf_op jit(solution)/shard_map/ppermute | solution.py:33
  37.7 6.2 %collective-permute-start = (bf16[32,256]{0,1:T(8,128)(2,1)S(1)}, bf16[32,256]{0,1:T(8,128)(2,1)S(1)}, u32[]{:S(2)}, u32[]{:S(2)}) collective-permute-start(bf16[32,256]{0,1:T(8,128)(2,1)S(1)} %get-tuple-element.10), channel_id=1, source_target_pairs={{0,1},{2,3},{4,5},{6,7},{8,9},{10,11},{12,13},{14,15},{16,17},{18,... | collective-permute-start | bytes 49160 | tf_op jit(solution)/shard_map/ppermute | solution.py:22
  41.3 6.0 %collective-permute-start.1 = (bf16[32,256]{0,1:T(8,128)(2,1)S(1)}, bf16[32,256]{0,1:T(8,128)(2,1)S(1)}, u32[]{:S(2)}, u32[]{:S(2)}) collective-permute-start(bf16[32,256]{0,1:T(8,128)(2,1)S(1)} %get-tuple-element.11), channel_id=1, source_target_pairs={{1,0},{3,2},{5,4},{7,6},{9,8},{11,10},{13,12},{15,14},{17,16},{19,... | collective-permute-start | bytes 49160 | tf_op jit(solution)/shard_map/ppermute | solution.py:25
  48.5 28.1 %copy-start.6 = (bf16[16]{0:T(256)(128)(2,1)S(1)}, bf16[16]{0:T(256)(128)(2,1)}, u32[]{:S(2)}) copy-start(bf16[16]{0:T(256)(128)(2,1)} %constant.53.clone.1) | copy-start | bytes 100
  48.5 10.7 %collective-permute-start.10 = (bf16[128,512]{0,1:T(8,128)(2,1)S(1)}, bf16[128,512]{0,1:T(8,128)(2,1)S(1)}, u32[]{:S(2)}, u32[]{:S(2)}) collective-permute-start(bf16[128,512]{0,1:T(8,128)(2,1)S(1)} %bitcast.87), channel_id=1, source_target_pairs={{0,8},{2,10},{4,12},{6,14},{8,16},{10,18},{12,20},{14,22},{16,24},... | collective-permute-start | bytes 393224 | tf_op jit(solution)/shard_map/ppermute | solution.py:33
  49.9 13.8 %collective-permute-start.11 = (bf16[128,512]{0,1:T(8,128)(2,1)S(1)}, bf16[128,512]{0,1:T(8,128)(2,1)S(1)}, u32[]{:S(2)}, u32[]{:S(2)}) collective-permute-start(bf16[128,512]{0,1:T(8,128)(2,1)S(1)} %bitcast.88), channel_id=1, source_target_pairs={{0,6},{2,8},{4,10},{6,12},{8,14},{10,16},{12,18},{14,20},{16,22},{... | collective-permute-start | bytes 393224 | tf_op jit(solution)/shard_map/ppermute | solution.py:33
  51.8 18.8 %collective-permute-start.12 = (bf16[128,512]{0,1:T(8,128)(2,1)S(1)}, bf16[128,512]{0,1:T(8,128)(2,1)S(1)}, u32[]{:S(2)}, u32[]{:S(2)}) collective-permute-start(bf16[128,512]{0,1:T(8,128)(2,1)S(1)} %bitcast.89), channel_id=1, source_target_pairs={{0,4},{2,6},{4,8},{6,10},{8,12},{10,14},{12,16},{14,18},{16,20},{1... | collective-permute-start | bytes 393224 | tf_op jit(solution)/shard_map/ppermute | solution.py:33
  53.8 20.8 %collective-permute-start.13 = (bf16[128,512]{0,1:T(8,128)(2,1)S(1)}, bf16[128,512]{0,1:T(8,128)(2,1)S(1)}, u32[]{:S(2)}, u32[]{:S(2)}) collective-permute-start(bf16[128,512]{0,1:T(8,128)(2,1)S(1)} %bitcast.90), channel_id=1, source_target_pairs={{0,2},{2,4},{4,6},{6,8},{8,10},{10,12},{12,14},{14,16},{16,18},{18... | collective-permute-start | bytes 393224 | tf_op jit(solution)/shard_map/ppermute | solution.py:33
  55.7 55.3 %collective-permute-start.2 = (bf16[128,512]{0,1:T(8,128)(2,1)S(1)}, bf16[128,512]{0,1:T(8,128)(2,1)S(1)}, u32[]{:S(2)}, u32[]{:S(2)}) collective-permute-start(bf16[128,512]{0,1:T(8,128)(2,1)S(1)} %bitcast.91), channel_id=1, source_target_pairs={{2,0},{4,2},{6,4},{8,6},{10,8},{12,10},{14,12},{16,14},{18,16},{20... | collective-permute-start | bytes 393224 | tf_op jit(solution)/shard_map/ppermute | solution.py:33
  59.2 20.3 %copy-start.1 = (bf16[128,512]{0,1:T(8,128)(2,1)}, bf16[128,512]{0,1:T(8,128)(2,1)S(1)}, u32[]{:S(2)}) copy-start(bf16[128,512]{0,1:T(8,128)(2,1)S(1)} %collective-permute-done.10) | copy-start | bytes 393220
  59.2 52.6 %collective-permute-start.3 = (bf16[128,512]{0,1:T(8,128)(2,1)S(1)}, bf16[128,512]{0,1:T(8,128)(2,1)S(1)}, u32[]{:S(2)}, u32[]{:S(2)}) collective-permute-start(bf16[128,512]{0,1:T(8,128)(2,1)S(1)} %bitcast.93), channel_id=1, source_target_pairs={{4,0},{6,2},{8,4},{10,6},{12,8},{14,10},{16,12},{18,14},{20,16},{2... | collective-permute-start | bytes 393224 | tf_op jit(solution)/shard_map/ppermute | solution.py:33
  63.8 15.7 %copy-start.2 = (bf16[128,512]{0,1:T(8,128)(2,1)}, bf16[128,512]{0,1:T(8,128)(2,1)S(1)}, u32[]{:S(2)}) copy-start(bf16[128,512]{0,1:T(8,128)(2,1)S(1)} %collective-permute-done.11) | copy-start | bytes 393220
  63.8 73.3 %collective-permute-start.4 = (bf16[128,512]{0,1:T(8,128)(2,1)S(1)}, bf16[128,512]{0,1:T(8,128)(2,1)}, u32[]{:S(2)}, u32[]{:S(2)}) collective-permute-start(bf16[128,512]{0,1:T(8,128)(2,1)S(1)} %bitcast.94), channel_id=1, source_target_pairs={{6,0},{8,2},{10,4},{12,6},{14,8},{16,10},{18,12},{20,14},{22,16},{... | collective-permute-start | bytes 393224 | tf_op jit(solution)/shard_map/ppermute | solution.py:33
  70.6 4.0 %copy-start.3 = (bf16[128,512]{0,1:T(8,128)(2,1)}, bf16[128,512]{0,1:T(8,128)(2,1)S(1)}, u32[]{:S(2)}) copy-start(bf16[128,512]{0,1:T(8,128)(2,1)S(1)} %collective-permute-done.12) | copy-start | bytes 393220
  70.6 68.0 %collective-permute-start.5 = (bf16[128,512]{0,1:T(8,128)(2,1)S(1)}, bf16[128,512]{0,1:T(8,128)(2,1)}, u32[]{:S(2)}, u32[]{:S(2)}) collective-permute-start(bf16[128,512]{0,1:T(8,128)(2,1)S(1)} %bitcast.95), channel_id=1, source_target_pairs={{8,0},{10,2},{12,4},{14,6},{16,8},{18,10},{20,12},{22,14},{24,16},... | collective-permute-start | bytes 393224 | tf_op jit(solution)/shard_map/ppermute | solution.py:33
  74.6 0.7 copy-start.4
  137.1 5.4 %copy-start.7 = (bf16[16]{0:T(256)(128)(2,1)S(1)}, bf16[16]{0:T(256)(128)(2,1)}, u32[]{:S(2)}) copy-start(bf16[16]{0:T(256)(128)(2,1)} %constant.53.clone.1) | copy-start | bytes 100
  164.9 1.6 copy-start.5
where the time goes:
time: 174 us; the launch traced here: 172 us
  local copies, waits for them, and re-layouts  84.7 us (49%)
  starting transfers between devices  53.3 us (31%)
  matrix products  14.8 us (9%)
  other arithmetic  14.7 us (8%)
  waiting for transfers between devices  3.49 us (2%)
    ppermute x16, starting transfers between devices, from_behind(): return lax.ppermute(value, axis, pairs)  48.9 us
    rev x1, local copies, waits for them, and re-layouts, stacks_from(): stacked = jnp.flip(stacked, axis=3)  20.2 us
    concatenate x12, local copies, waits for them, and re-layouts, cross_terms(): jnp.concatenate(partners, axis=1).reshape(bin_count, -1, 2, WINDOWS)  17.8 us
    unnamed x26, local copies, waits for them, and re-layouts  11.3 us
    dot_general x2, local copies, waits for them, and re-layouts, cross_terms(): jnp.einsum('kiv,kjv->kij', left_conj, right_swap, preferred_element_type=...  8.54 us
    dot_general x2, local copies, waits for them, and re-layouts, cross_terms(): jnp.einsum('kiv,kjv->kij', left_rows, right_same, preferred_element_type=...  8.54 us
    reshape x6, local copies, waits for them, and re-layouts, skew_take(): flattened.reshape(leading + (row_count, col_count + 1))[..., :reach_cols]  6.85 us
    another operation x4, other arithmetic, stacks_from(): jnp.stack([skew_take(real_part, offset, REACH) / divisor, skew_take(imag_...  5.62 us
  transfers between devices with their start and end apart: 18, of which 1 were waited for; matrix products, arithmetic and copies ran while one was open for 45% of the time, Pallas kernels for 0%

commit v1 on v0

v1 whole, which is shorter than its diff:
```python
import functools
import math

import jax
import jax.numpy as jnp
import ml_dtypes
import numpy as np
from jax import lax
from jax.experimental import pallas as pl
from jax.experimental.pallas import tpu as pltpu
from jax.sharding import PartitionSpec as P

WINDOWS = 8
BINS = 256
REACH = 128
TIME_HALF = 128
BIN_HALF = 32
LANES = 128
PACK = LANES // (2 * WINDOWS)
STEP = 2
VMEM_BYTES = 40 * 1024 * 1024


def bin_columns(bin_count):
    halo = np.concatenate([np.arange(-BIN_HALF, 0), np.arange(bin_count, bin_count + BIN_HALF)])
    own = np.arange(bin_count).reshape(-1, 1, PACK)
    parts = np.arange(2).reshape(1, 2, 1)
    shape = (bin_count // PACK, 2, PACK)
    bins = np.concatenate([halo, halo, np.broadcast_to(own, shape).ravel()])
    part = np.concatenate(
        [np.zeros_like(halo), np.ones_like(halo), np.broadcast_to(parts, shape).ravel()]
    )
    return bins, part


def dft_tables(freq_devices, samples):
    bin_count = BINS // freq_devices
    bins, part = bin_columns(bin_count)
    sample_ids = np.arange(samples)
    tables = []
    for device in range(freq_devices):
        freq = device * bin_count + bins + 1
        inside = (freq >= 1) & (freq <= BINS)
        turn = (freq[None, :] * sample_ids[:, None]) % samples
        phase = turn.astype(np.float32) * np.float32(2.0 * math.pi / samples)
        wave = np.where(part[None, :] == 0, np.cos(phase), -np.sin(phase)).astype(np.float32)
        wave = wave * np.float32(1.0 / math.sqrt(samples)) * inside[None, :]
        tables.append(wave.astype(ml_dtypes.bfloat16))
    return np.stack(tables)


def smoother(bin_count):
    bins, _ = bin_columns(bin_count)
    own = bins[4 * BIN_HALF :]
    return (np.abs(bins[:, None] - own[None, :]) <= BIN_HALF).astype(ml_dtypes.bfloat16)


def whiten_kernel(x_ref, ok_ref, win_ref, table_ref, smooth_ref, out_ref, mag_ref, spec_ref):
    channels, windows, samples = x_ref.shape
    rows = channels * windows
    halo = 4 * BIN_HALF
    own = table_ref.shape[1] - halo
    tile = 2 * TIME_HALF
    count = 2 * TIME_HALF + 1

    mag_ref[:, :TIME_HALF] = jnp.zeros((rows, TIME_HALF), jnp.bfloat16)
    mag_ref[:, TIME_HALF + samples :] = jnp.zeros((rows, TIME_HALF), jnp.bfloat16)
    for t in range(samples // tile):
        x = x_ref[:, :, t * tile : (t + 1) * tile].astype(jnp.float32).reshape(rows, tile)
        mag_ref[:, TIME_HALF + t * tile : TIME_HALF + (t + 1) * tile] = jnp.abs(x).astype(
            jnp.bfloat16
        )
    source = lax.broadcasted_iota(jnp.int32, (2 * tile, tile), 0) - TIME_HALF
    target = lax.broadcasted_iota(jnp.int32, (2 * tile, tile), 1)
    band = (jnp.abs(source - target) <= TIME_HALF).astype(jnp.float32).astype(jnp.bfloat16)
    spectra = jnp.zeros((rows, own + halo), jnp.float32)
    for t in range(samples // tile):
        sums = jnp.dot(
            mag_ref[:, t * tile : (t + 2) * tile], band, preferred_element_type=jnp.float32
        )
        x = x_ref[:, :, t * tile : (t + 1) * tile].astype(jnp.float32).reshape(rows, tile)
        leveled = (x * (count / (sums + count * 1e-06))).astype(jnp.bfloat16)
        spectra = spectra + jnp.dot(
            leveled, table_ref[t * tile : (t + 1) * tile, :], preferred_element_type=jnp.float32
        )

    power = spectra * spectra
    high = power.astype(jnp.bfloat16)
    low = (power - high.astype(jnp.float32)).astype(jnp.bfloat16)
    ones = smooth_ref[...]
    smooth = jnp.dot(high, ones, preferred_element_type=jnp.float32) + jnp.dot(
        low, ones, preferred_element_type=jnp.float32
    )
    white = spectra[:, halo:] * lax.rsqrt(smooth * (1.0 / (2 * BIN_HALF + 1)) + 1e-06)
    for t in range(0, own, LANES):
        width = min(LANES, own - t)
        spec_ref[t // LANES, :, :width] = white[:, t : t + width]

    flags = (ok_ref[...] * win_ref[...]).astype(jnp.float32).astype(jnp.bfloat16)
    lane = lax.broadcasted_iota(jnp.int32, (windows, LANES), 1)
    window = lax.broadcasted_iota(jnp.int32, (windows, LANES), 0)
    contract = (((0,), (0,)), ((), ()))
    picked = (lane == window).astype(jnp.float32).astype(jnp.bfloat16)
    out_ref[:, windows * own :] = lax.dot_general(
        flags, picked, contract, preferred_element_type=jnp.float32
    ).astype(jnp.bfloat16)
    spread = (lane // (2 * PACK) == window).astype(jnp.float32).astype(jnp.bfloat16)
    usable = lax.dot_general(flags, spread, contract, preferred_element_type=jnp.float32)

    width = 2 * PACK
    for g in range(own // width):
        pieces = [
            spec_ref[g * width // LANES, pl.ds(w, channels, stride=windows), :][
                :, g * width % LANES : g * width % LANES + width
            ]
            for w in range(windows)
        ]
        packed = jnp.concatenate(pieces, axis=1) * usable
        out_ref[:, g * LANES : (g + 1) * LANES] = packed.astype(jnp.bfloat16)


def whiten(strain, channel_ok, window_ok, freq_devices):
    channels, windows, samples = strain.shape
    bin_count = BINS // freq_devices
    tables = jnp.asarray(dft_tables(freq_devices, samples))
    ones = jnp.asarray(smoother(bin_count))
    columns = tables.shape[2]
    own = 2 * bin_count
    whole = lambda *shape: pl.BlockSpec(shape, lambda i, q: (0,) * len(shape))
    return pl.pallas_call(
        lambda q_ref, *refs: whiten_kernel(*refs),
        grid_spec=pltpu.PrefetchScalarGridSpec(
            num_scalar_prefetch=1,
            grid=(1,),
            in_specs=[
                whole(channels, windows, samples),
                whole(1, channels),
                whole(windows, channels),
                pl.BlockSpec((None, samples, columns), lambda i, q: (q[0], 0, 0)),
                whole(columns, own),
            ],
            out_specs=whole(channels, windows * own + LANES),
            scratch_shapes=[
                pltpu.VMEM((channels * windows, samples + 2 * TIME_HALF), jnp.bfloat16),
                pltpu.VMEM((-(-own // LANES), channels * windows, LANES), jnp.float32),
            ],
        ),
        out_shape=jax.ShapeDtypeStruct((channels, windows * own + LANES), jnp.bfloat16),
        compiler_params=pltpu.CompilerParams(vmem_limit_bytes=VMEM_BYTES),
        name="whiten",
    )(
        lax.axis_index("freq").reshape(1).astype(jnp.int32),
        strain,
        channel_ok.reshape(1, channels),
        window_ok.T,
        tables,
        ones,
    )


def trade(value, partner):
    count = lax.axis_size("ch")
    pairs = [(i, partner(i)) for i in range(count) if 0 <= partner(i) < count]
    return lax.ppermute(value, "ch", pairs)


def beside(i):
    return i ^ 1


def near(i):
    k, core = i // 2, i % 2
    step = 1 - 2 * ((k + core) % 2)
    return 2 * (k + step) + core


def far(i):
    k, core = i // 2, i % 2
    step = 2 - 4 * ((k // 2 + core) % 2)
    return 2 * (k + step) + core


def cross_kernel(
    own_ref, mate_ref, near_ref, far_ref, near2_ref, far2_ref,
    own_u, mate_u, near_u, far_u, near2_u, far2_u,
    ahead_ref, behind_ref, div_ahead, div_behind,
):
    channels = own_ref.shape[0]
    index = lax.axis_index("ch")
    core = lax.rem(index, 2)
    pair = index // 2
    near_up = lax.rem(pair + core, 2) == 0
    far_up = lax.rem(pair // 2 + core, 2) == 0
    first = core == 0

    def neighbours(own, mate, near, far, near2, far2):
        def ordered(mine, theirs, up):
            block = jnp.where(up, mine, theirs)
            low, high = block[:channels], block[channels:]
            keep = first == up
            return jnp.where(keep, low, high), jnp.where(keep, high, low)

        up1 = ordered(near, near2, near_up)
        down1 = ordered(near, near2, jnp.logical_not(near_up))
        up2 = ordered(far, far2, far_up)
        down2 = ordered(far, far2, jnp.logical_not(far_up))
        pick = lambda a, b: jnp.where(first, a, b)
        ahead = [own, pick(mate, up1[0]), pick(up1[0], up1[1]), pick(up1[1], up2[0]), pick(up2[0], up2[1])]
        behind = [pick(down2[0], down2[1]), pick(down2[1], down1[0]), pick(down1[0], down1[1]), pick(down1[1], mate), own]
        return jnp.concatenate(ahead, axis=0), jnp.concatenate(behind, axis=0)

    total = REACH + channels
    fold = lax.broadcasted_iota(jnp.int32, (total, total), 0)
    source = lax.broadcasted_iota(jnp.int32, (total, total), 1)
    lead = 2 * channels - 1
    wanted = jnp.where(
        fold < channels,
        lead - fold,
        jnp.where(fold < REACH, REACH + lead - fold, REACH + channels - 1 - fold),
    )
    turn = (wanted == source).astype(jnp.float32).astype(jnp.bfloat16)

    def arranged(rows_ahead, rows_behind):
        turned = jnp.dot(turn, rows_behind, preferred_element_type=jnp.float32).astype(jnp.bfloat16)
        return jnp.concatenate(
            [rows_ahead[:REACH], turned[:REACH], rows_ahead[REACH:], turned[REACH:]], axis=0
        )

    row = lax.broadcasted_iota(jnp.int32, (channels, LANES), 0)
    lane = lax.broadcasted_iota(jnp.int32, (channels, LANES), 1)
    wrap_ahead = lane <= row
    wrap_behind = (lane >= channels) & (lane <= lead - row)
    flip = 7 - lax.broadcasted_iota(jnp.int32, (8, LANES), 0)

    def turned_rows(v):
        return jnp.take_along_axis(v, flip, axis=0)

    def skewed(product):
        ends = jnp.concatenate(
            [product[:, 2 * REACH :], jnp.zeros((channels, REACH - 2 * channels), jnp.float32)], axis=1
        )
        a = jnp.where(wrap_ahead, ends, product[:, :REACH])
        b = jnp.where(wrap_behind, ends, product[:, REACH : 2 * REACH])
        aheads = []
        for r in range(0, channels, 8):
            v = pltpu.roll(turned_rows(a[r : r + 8]), (2 * LANES - r - 8) % LANES, 1, stride=1, stride_axis=0)
            aheads.append(turned_rows(v))
        b = pltpu.roll(b, 2 * LANES - 2 * channels - LANES, 1, stride=1, stride_axis=0)
        return jnp.concatenate(aheads, axis=0), b

    contract = (((1,), (1,)), ((), ()))

    @pl.when(pl.program_id(0) == 0)
    def _():
        rhs = arranged(*neighbours(*(r[...] for r in (own_u, mate_u, near_u, far_u, near2_u, far2_u))))
        counts = lax.dot_general(own_u[...], rhs, contract, preferred_element_type=jnp.float32)
        ahead, behind = skewed(counts)
        div_ahead[...] = 1.0 / jnp.maximum(ahead, 1.0)
        div_behind[...] = 1.0 / jnp.maximum(behind, 1.0)

    rows_ahead, rows_behind = neighbours(
        *(r[...] for r in (own_ref, mate_ref, near_ref, far_ref, near2_ref, far2_ref))
    )
    rhs = arranged(rows_ahead, rows_behind)
    for s in range(STEP):
        lanes = slice(s * LANES, (s + 1) * LANES)
        a = own_ref[:, lanes].astype(jnp.float32)
        part = lax.rem(lane // PACK, 2)
        rotated = jnp.where(part == 0, -pltpu.roll(a, LANES - PACK, 1), pltpu.roll(a, PACK, 1))
        zero = jnp.zeros_like(a)
        rows = []
        for f in range(PACK):
            mask = lax.rem(lane, PACK) == f
            rows += [jnp.where(mask, a, zero), jnp.where(mask, rotated, zero)]
        lhs = jnp.concatenate(rows, axis=0).astype(jnp.bfloat16)
        product = lax.dot_general(lhs, rhs[:, lanes], contract, preferred_element_type=jnp.float32)
        for f in range(PACK):
            for v in range(2):
                start = (2 * f + v) * channels
                ahead, behind = skewed(product[start : start + channels])
                ahead_ref[v, s * PACK + f] = (ahead * div_ahead[...]).astype(jnp.bfloat16)
                behind_ref[v, s * PACK + f] = (behind * div_behind[...]).astype(jnp.bfloat16)


def cross(own, mate, near_rows, far_rows, near2, far2, bin_count):
    channels = own.shape[0]
    width = STEP * LANES
    usable_at = bin_count // PACK
    values = [own, mate, near_rows, far_rows, near2, far2]
    specs = [pl.BlockSpec((v.shape[0], width), lambda g: (0, g)) for v in values]
    flags = [pl.BlockSpec((v.shape[0], LANES), lambda g: (0, usable_at)) for v in values]
    out = pl.BlockSpec((2, STEP * PACK, channels, REACH), lambda g: (0, g, 0, 0))
    shape = jax.ShapeDtypeStruct((2, bin_count, channels, REACH), jnp.bfloat16)
    return pl.pallas_call(
        cross_kernel,
        grid=(bin_count // (STEP * PACK),),
        in_specs=specs + flags,
        out_specs=[out, out],
        out_shape=[shape, shape],
        scratch_shapes=[pltpu.VMEM((channels, REACH), jnp.float32)] * 2,
        compiler_params=pltpu.CompilerParams(vmem_limit_bytes=VMEM_BYTES),
        name="cross",
    )(*values, *values)


def per_device(strain, channel_ok, window_ok):
    freq_devices = lax.axis_size("freq")
    own = whiten(strain, channel_ok, window_ok, freq_devices)
    mate = trade(own, beside)
    both = jnp.concatenate([own, mate], axis=0)
    near_rows = trade(both, near)
    far_rows = trade(both, far)
    near2 = trade(near_rows, beside)
    far2 = trade(far_rows, beside)
    return cross(own, mate, near_rows, far_rows, near2, far2, BINS // freq_devices)


def solution(mesh):
    return jax.shard_map(
        per_device,
        mesh=mesh,
        in_specs=(P("ch", None, None), P("ch"), P("ch", None)),
        out_specs=(P(None, "freq", "ch", None), P(None, "freq", "ch", None)),
        check_vma=False,
    )
```

time: 174 us -> 36 us (0.21)
  the two profiles are of different devices: /device:TPU:25 before, /device:TPU:17 now
where the time goes in v1:
time: 36 us; the launch traced here: 35.7 us
  starting transfers between devices  12.5 us (35%)
  Pallas kernels  11.8 us (33%)
  local copies, waits for them, and re-layouts  5.38 us (15%)
  waiting for transfers between devices  5.34 us (15%)
  between operations  0.67 us (2%)
    ppermute x5, starting transfers between devices, trade(): return lax.ppermute(value, 'ch', pairs)  12.5 us
    pallas_call x1, Pallas kernels, cross(): pl.pallas_call(cross_kernel, grid=(bin_count // (STEP * PACK),), in_specs...  8.57 us
    unnamed x10, local copies, waits for them, and re-layouts  5.38 us
    ppermute x5, waiting for transfers between devices, trade(): return lax.ppermute(value, 'ch', pairs)  5.34 us
    pallas_call x1, Pallas kernels, whiten(): pl.pallas_call(lambda q_ref, *refs: whiten_kernel(*refs), grid_spec=pltpu...  3.19 us
  transfers between devices with their start and end apart: 5, of which 4 were waited for; matrix products, arithmetic and copies ran while one was open for 0% of the time, Pallas kernels for 0%

profile of v1, /device:TPU:17, one launch (start us, length us, event | category | flops | bytes accessed | tf_op | source)
XLA Modules:
  0.0 35.7 jit_solution(7036741697079943501)
XLA Ops:
  0.6 0.0 copy-start
  0.6 1.9 %copy-done = bf16[2,2048,384]{2,1,0:T(8,128)(2,1)S(1)} copy-done((bf16[2,2048,384]{2,1,0:T(8,128)(2,1)S(1)}, bf16[2,2048,384]{2,1,0:T(8,128)(2,1)}, u32[]{:S(2)}) %copy-start) | copy-done | bytes 3145752
  2.5 0.0 copy-start.1
  2.5 1.2 %copy-done.1 = bf16[32,8,2048]{2,1,0:T(8,128)(2,1)S(1)} copy-done((bf16[32,8,2048]{2,1,0:T(8,128)(2,1)S(1)}, bf16[32,8,2048]{2,1,0:T(8,128)(2,1)}, u32[]{:S(2)}) %copy-start.1) | copy-done | bytes 1048600
  3.8 0.0 copy-start.2
  3.8 0.9 %copy-done.2 = bf16[384,256]{1,0:T(8,128)(2,1)S(1)} copy-done((bf16[384,256]{1,0:T(8,128)(2,1)S(1)}, bf16[384,256]{1,0:T(8,128)(2,1)}, u32[]{:S(2)}) %copy-start.2) | copy-done | bytes 196632
  4.7 0.0 copy-start.3
  4.7 0.7 %copy-done.3 = s32[32,8]{0,1:T(8,128)S(1)} copy-done((s32[32,8]{0,1:T(8,128)S(1)}, s32[32,8]{0,1:T(8,128)}, u32[]{:S(2)}) %copy-start.3) | copy-done | bytes 1048
  5.4 0.0 copy-start.4
  5.4 0.7 %copy-done.4 = s32[32]{0:T(128)S(1)} copy-done((s32[32]{0:T(128)S(1)}, s32[32]{0:T(128)}, u32[]{:S(2)}) %copy-start.4) | copy-done | bytes 152
  6.0 3.2 %whiten.1.own_ref.own_u = bf16[32,2176]{1,0:T(8,128)(2,1)S(1)} custom-call(s32[1]{0:T(128)} %bitcast.q_ref, bf16[32,8,2048]{2,1,0:T(8,128)(2,1)S(1)} %copy-done.1, s32[1,32]{1,0:T(1,128)S(1)} %bitcast.4, s32[8,32]{1,0:T(8,128)S(1)} %bitcast.3, bf16[2,2048,384]{2,1,0:T(8,128)(2,1)S(1)} %copy-done, bf16[384,256]{1,0:T(8,128)(2,1)S(1)} %copy-done.2), custom_call_target="tpu_custom_call" | custom-call | tf_op jit(solution)/shard_map/whiten/pallas_call | solution.py:130
  9.2 0.7 %collective-permute-start = (bf16[32,2176]{1,0:T(8,128)(2,1)S(1)}, bf16[32,2176]{1,0:T(8,128)(2,1)S(1)}, u32[]{:S(2)}, u32[]{:S(2)}) collective-permute-start(bf16[32,2176]{1,0:T(8,128)(2,1)S(1)} %whiten.1.own_ref.own_u), channel_id=1, source_target_pairs={{0,2},{2,0},{4,6},{6,4},{8,10},{10,8},{12,14},{14,12},{16,18},{18,... | collective-permute-start | bytes 417800 | tf_op jit(solution)/shard_map/ppermute | solution.py:164
  10.0 1.0 %collective-permute-done.mate_ref.mate_u = bf16[32,2176]{1,0:T(8,128)(2,1)S(1)} collective-permute-done((bf16[32,2176]{1,0:T(8,128)(2,1)S(1)}, bf16[32,2176]{1,0:T(8,128)(2,1)S(1)}, u32[]{:S(2)}, u32[]{:S(2)}) %collective-permute-start) | collective-permute-done | bytes 139296 | tf_op jit(solution)/shard_map/ppermute | solution.py:164
  11.0 2.1 %collective-permute-start.2 = (bf16[64,2176]{1,0:T(8,128)(2,1)S(1)}, bf16[64,2176]{1,0:T(8,128)(2,1)S(1)}, u32[]{:S(2)}, u32[]{:S(2)}) collective-permute-start(bf16[64,2176]{1,0:T(8,128)(2,1)S(1)} %pad_maximum_fusion), channel_id=1, source_target_pairs={{0,8},{4,12},{8,0},{10,18},{12,4},{14,22},{16,24},{18,10},{20,28},... | collective-permute-start | bytes 835592 | tf_op jit(solution)/shard_map/ppermute | solution.py:164
  13.1 4.2 %collective-permute-start.1 = (bf16[64,2176]{1,0:T(8,128)(2,1)S(1)}, bf16[64,2176]{1,0:T(8,128)(2,1)S(1)}, u32[]{:S(2)}, u32[]{:S(2)}) collective-permute-start(bf16[64,2176]{1,0:T(8,128)(2,1)S(1)} %pad_maximum_fusion), channel_id=1, source_target_pairs={{0,4},{4,0},{6,10},{8,12},{10,6},{12,8},{14,18},{16,20},{18,14},{2... | collective-permute-start | bytes 835592 | tf_op jit(solution)/shard_map/ppermute | solution.py:164
  17.2 1.3 %collective-permute-done.2.far_ref.far_u = bf16[64,2176]{1,0:T(8,128)(2,1)S(1)} collective-permute-done((bf16[64,2176]{1,0:T(8,128)(2,1)S(1)}, bf16[64,2176]{1,0:T(8,128)(2,1)S(1)}, u32[]{:S(2)}, u32[]{:S(2)}) %collective-permute-start.2) | collective-permute-done | bytes 278560 | tf_op jit(solution)/shard_map/ppermute | solution.py:164
  18.6 1.9 %collective-permute-start.4 = (bf16[64,2176]{1,0:T(8,128)(2,1)S(1)}, bf16[64,2176]{1,0:T(8,128)(2,1)S(1)}, u32[]{:S(2)}, u32[]{:S(2)}) collective-permute-start(bf16[64,2176]{1,0:T(8,128)(2,1)S(1)} %collective-permute-done.2.far_ref.far_u), channel_id=1, source_target_pairs={{0,2},{2,0},{4,6},{6,4},{8,10},{10,8},{12,14},{14,12},{16,18},{18,... | collective-permute-start | bytes 835592 | tf_op jit(solution)/shard_map/ppermute | solution.py:164
  20.5 1.8 %collective-permute-done.1.near_ref.near_u = bf16[64,2176]{1,0:T(8,128)(2,1)S(1)} collective-permute-done((bf16[64,2176]{1,0:T(8,128)(2,1)S(1)}, bf16[64,2176]{1,0:T(8,128)(2,1)S(1)}, u32[]{:S(2)}, u32[]{:S(2)}) %collective-permute-start.1) | collective-permute-done | bytes 278560 | tf_op jit(solution)/shard_map/ppermute | solution.py:164
  22.3 3.6 %collective-permute-start.3 = (bf16[64,2176]{1,0:T(8,128)(2,1)S(1)}, bf16[64,2176]{1,0:T(8,128)(2,1)S(1)}, u32[]{:S(2)}, u32[]{:S(2)}) collective-permute-start(bf16[64,2176]{1,0:T(8,128)(2,1)S(1)} %collective-permute-done.1.near_ref.near_u), channel_id=1, source_target_pairs={{0,2},{2,0},{4,6},{6,4},{8,10},{10,8},{12,14},{14,12},{16,18},{18,... | collective-permute-start | bytes 835592 | tf_op jit(solution)/shard_map/ppermute | solution.py:164
  25.9 0.0 collective-permute-done.4.far2_ref.far2_u
  25.9 1.2 %collective-permute-done.3.near2_ref.near2_u = bf16[64,2176]{1,0:T(8,128)(2,1)S(1)} collective-permute-done((bf16[64,2176]{1,0:T(8,128)(2,1)S(1)}, bf16[64,2176]{1,0:T(8,128)(2,1)S(1)}, u32[]{:S(2)}, u32[]{:S(2)}) %collective-permute-start.3) | collective-permute-done | bytes 278560 | tf_op jit(solution)/shard_map/ppermute | solution.py:164
  27.1 8.6 %cross.1 = (bf16[2,128,32,128]{3,2,1,0:T(8,128)(2,1)}, bf16[2,128,32,128]{3,2,1,0:T(8,128)(2,1)}) custom-call(bf16[32,2176]{1,0:T(8,128)(2,1)S(1)} %whiten.1.own_ref.own_u, bf16[32,2176]{1,0:T(8,128)(2,1)S(1)} %collective-permute-done.mate_ref.mate_u, bf16[64,2176]{1,0:T(8,128)(2,1)S(1)} %collective-permute-done.1.near_ref.near_u, ...), custom_call_target="tpu_custom_call" | custom-call | tf_op jit(solution)/shard_map/cross/pallas_call | solution.py:294
  (1 shorter events, 0.0 us)
Async XLA Ops:
  0.6 1.9 %copy-start = (bf16[2,2048,384]{2,1,0:T(8,128)(2,1)S(1)}, bf16[2,2048,384]{2,1,0:T(8,128)(2,1)}, u32[]{:S(2)}) copy-start(bf16[2,2048,384]{2,1,0:T(8,128)(2,1)} %constant.8.clone.refs_3_) | copy-start | bytes 9437188
  2.5 1.2 %copy-start.1 = (bf16[32,8,2048]{2,1,0:T(8,128)(2,1)S(1)}, bf16[32,8,2048]{2,1,0:T(8,128)(2,1)}, u32[]{:S(2)}) copy-start(bf16[32,8,2048]{2,1,0:T(8,128)(2,1)} %refs_0_.1) | copy-start | bytes 3145732
  3.8 0.9 %copy-start.2 = (bf16[384,256]{1,0:T(8,128)(2,1)S(1)}, bf16[384,256]{1,0:T(8,128)(2,1)}, u32[]{:S(2)}) copy-start(bf16[384,256]{1,0:T(8,128)(2,1)} %constant.9.clone.refs_4_) | copy-start | bytes 589828
  4.7 0.7 %copy-start.3 = (s32[32,8]{0,1:T(8,128)S(1)}, s32[32,8]{0,1:T(8,128)}, u32[]{:S(2)}) copy-start(s32[32,8]{0,1:T(8,128)} %param.7) | copy-start | bytes 3076
  5.4 0.7 %copy-start.4 = (s32[32]{0:T(128)S(1)}, s32[32]{0:T(128)}, u32[]{:S(2)}) copy-start(s32[32]{0:T(128)} %param.6) | copy-start | bytes 388
  9.2 1.7 %collective-permute-start = (bf16[32,2176]{1,0:T(8,128)(2,1)S(1)}, bf16[32,2176]{1,0:T(8,128)(2,1)S(1)}, u32[]{:S(2)}, u32[]{:S(2)}) collective-permute-start(bf16[32,2176]{1,0:T(8,128)(2,1)S(1)} %whiten.1.own_ref.own_u), channel_id=1, source_target_pairs={{0,2},{2,0},{4,6},{6,4},{8,10},{10,8},{12,14},{14,12},{16,18},{18,... | collective-permute-start | bytes 417800 | tf_op jit(solution)/shard_map/ppermute | solution.py:164
  11.0 7.6 %collective-permute-start.2 = (bf16[64,2176]{1,0:T(8,128)(2,1)S(1)}, bf16[64,2176]{1,0:T(8,128)(2,1)S(1)}, u32[]{:S(2)}, u32[]{:S(2)}) collective-permute-start(bf16[64,2176]{1,0:T(8,128)(2,1)S(1)} %pad_maximum_fusion), channel_id=1, source_target_pairs={{0,8},{4,12},{8,0},{10,18},{12,4},{14,22},{16,24},{18,10},{20,28},... | collective-permute-start | bytes 835592 | tf_op jit(solution)/shard_map/ppermute | solution.py:164
  13.1 9.3 %collective-permute-start.1 = (bf16[64,2176]{1,0:T(8,128)(2,1)S(1)}, bf16[64,2176]{1,0:T(8,128)(2,1)S(1)}, u32[]{:S(2)}, u32[]{:S(2)}) collective-permute-start(bf16[64,2176]{1,0:T(8,128)(2,1)S(1)} %pad_maximum_fusion), channel_id=1, source_target_pairs={{0,4},{4,0},{6,10},{8,12},{10,6},{12,8},{14,18},{16,20},{18,14},{2... | collective-permute-start | bytes 835592 | tf_op jit(solution)/shard_map/ppermute | solution.py:164
  18.6 7.3 %collective-permute-start.4 = (bf16[64,2176]{1,0:T(8,128)(2,1)S(1)}, bf16[64,2176]{1,0:T(8,128)(2,1)S(1)}, u32[]{:S(2)}, u32[]{:S(2)}) collective-permute-start(bf16[64,2176]{1,0:T(8,128)(2,1)S(1)} %collective-permute-done.2.far_ref.far_u), channel_id=1, source_target_pairs={{0,2},{2,0},{4,6},{6,4},{8,10},{10,8},{12,14},{14,12},{16,18},{18,... | collective-permute-start | bytes 835592 | tf_op jit(solution)/shard_map/ppermute | solution.py:164
  22.3 4.8 %collective-permute-start.3 = (bf16[64,2176]{1,0:T(8,128)(2,1)S(1)}, bf16[64,2176]{1,0:T(8,128)(2,1)S(1)}, u32[]{:S(2)}, u32[]{:S(2)}) collective-permute-start(bf16[64,2176]{1,0:T(8,128)(2,1)S(1)} %collective-permute-done.1.near_ref.near_u), channel_id=1, source_target_pairs={{0,2},{2,0},{4,6},{6,4},{8,10},{10,8},{12,14},{14,12},{16,18},{18,... | collective-permute-start | bytes 835592 | tf_op jit(solution)/shard_map/ppermute | solution.py:164

commit v2 on v1

v2 whole, which is shorter than its diff:
```python
import functools
import math

import jax
import jax.numpy as jnp
import ml_dtypes
import numpy as np
from jax import lax
from jax.experimental import pallas as pl
from jax.experimental.pallas import tpu as pltpu
from jax.sharding import PartitionSpec as P

WINDOWS = 8
BINS = 256
REACH = 128
TIME_HALF = 128
BIN_HALF = 32
LANES = 128
PACK = LANES // (2 * WINDOWS)
CHUNK = 2048
WIDE = 512
VMEM_BYTES = 40 * 1024 * 1024


def bin_columns(bin_count):
    halo = np.concatenate([np.arange(-BIN_HALF, 0), np.arange(bin_count, bin_count + BIN_HALF)])
    own = np.arange(bin_count).reshape(-1, 1, PACK)
    parts = np.arange(2).reshape(1, 2, 1)
    shape = (bin_count // PACK, 2, PACK)
    bins = np.concatenate([halo, halo, np.broadcast_to(own, shape).ravel()])
    part = np.concatenate(
        [np.zeros_like(halo), np.ones_like(halo), np.broadcast_to(parts, shape).ravel()]
    )
    return bins, part


def dft_tables(freq_devices, samples):
    bin_count = BINS // freq_devices
    bins, part = bin_columns(bin_count)
    sample_ids = np.arange(samples)
    tables = []
    for device in range(freq_devices):
        freq = device * bin_count + bins + 1
        inside = (freq >= 1) & (freq <= BINS)
        turn = (freq[None, :] * sample_ids[:, None]) % samples
        phase = turn.astype(np.float32) * np.float32(2.0 * math.pi / samples)
        wave = np.where(part[None, :] == 0, np.cos(phase), -np.sin(phase)).astype(np.float32)
        wave = wave * np.float32(1.0 / math.sqrt(samples)) * inside[None, :]
        tables.append(wave.astype(ml_dtypes.bfloat16))
    return np.stack(tables)


def smoother(bin_count):
    bins, _ = bin_columns(bin_count)
    own = bins[4 * BIN_HALF :]
    return (np.abs(bins[:, None] - own[None, :]) <= BIN_HALF).astype(ml_dtypes.bfloat16)


def whiten_kernel(
    x_hbm, ok_hbm, win_hbm, table_hbm, smooth_hbm, out_ref,
    x_ref, ok_ref, win_ref, table_ref, smooth_ref, mag_ref, level_ref, spec_ref, x_sems, table_sems, sems,
):
    channels, windows, samples = x_ref.shape
    rows = channels * windows
    halo = 4 * BIN_HALF
    own = table_ref.shape[1] - halo
    tile = 2 * TIME_HALF
    count = 2 * TIME_HALF + 1
    tiles = samples // tile
    q = lax.axis_index("freq")

    def chunk(k):
        return pl.ds(k * CHUNK, CHUNK)

    x_copies = [
        pltpu.make_async_copy(x_hbm.at[:, :, chunk(k)], x_ref.at[:, :, chunk(k)], x_sems.at[k])
        for k in range(samples // CHUNK)
    ]
    table_copies = [
        pltpu.make_async_copy(table_hbm.at[q, chunk(k)], table_ref.at[chunk(k)], table_sems.at[k])
        for k in range(samples // CHUNK)
    ]
    small_copies = [
        pltpu.make_async_copy(source, target, sems.at[k])
        for k, (source, target) in enumerate(
            ((ok_hbm, ok_ref), (win_hbm, win_ref), (smooth_hbm, smooth_ref))
        )
    ]
    for copy in x_copies + table_copies + small_copies:
        copy.start()

    mag_ref[:, :TIME_HALF] = jnp.zeros((rows, TIME_HALF), jnp.bfloat16)
    mag_ref[:, TIME_HALF + samples :] = jnp.zeros((rows, TIME_HALF), jnp.bfloat16)
    source = lax.broadcasted_iota(jnp.int32, (2 * tile, tile), 0) - TIME_HALF
    target = lax.broadcasted_iota(jnp.int32, (2 * tile, tile), 1)
    band = (jnp.abs(source - target) <= TIME_HALF).astype(jnp.float32).astype(jnp.bfloat16)

    def loaded(t):
        return x_ref[:, :, t * tile : (t + 1) * tile].astype(jnp.float32).reshape(rows, tile)

    for t in range(tiles):
        if t * tile % CHUNK == 0:
            x_copies[t * tile // CHUNK].wait()
        mag_ref[:, TIME_HALF + t * tile : TIME_HALF + (t + 1) * tile] = jnp.abs(loaded(t)).astype(
            jnp.bfloat16
        )
    for t in range(tiles):
        sums = jnp.dot(
            mag_ref[:, t * tile : (t + 2) * tile], band, preferred_element_type=jnp.float32
        )
        level_ref[:, t * tile : (t + 1) * tile] = (
            loaded(t) * (count / (sums + count * 1e-06))
        ).astype(jnp.bfloat16)
    for copy in table_copies + small_copies:
        copy.wait()
    spectra = jnp.dot(level_ref[...], table_ref[...], preferred_element_type=jnp.float32)

    power = spectra * spectra
    high = power.astype(jnp.bfloat16)
    low = (power - high.astype(jnp.float32)).astype(jnp.bfloat16)
    ones = smooth_ref[...]
    smooth = jnp.dot(high, ones, preferred_element_type=jnp.float32) + jnp.dot(
        low, ones, preferred_element_type=jnp.float32
    )
    white = spectra[:, halo:] * lax.rsqrt(smooth * (1.0 / (2 * BIN_HALF + 1)) + 1e-06)
    for t in range(0, own, LANES):
        width = min(LANES, own - t)
        spec_ref[t // LANES, :, :width] = white[:, t : t + width]

    flags = (ok_ref[...] * win_ref[...]).astype(jnp.float32).astype(jnp.bfloat16)
    lane = lax.broadcasted_iota(jnp.int32, (windows, LANES), 1)
    window = lax.broadcasted_iota(jnp.int32, (windows, LANES), 0)
    contract = (((0,), (0,)), ((), ()))
    picked = (lane == window).astype(jnp.float32).astype(jnp.bfloat16)
    out_ref[:, windows * own :] = lax.dot_general(
        flags, picked, contract, preferred_element_type=jnp.float32
    ).astype(jnp.bfloat16)
    spread = (lane // (2 * PACK) == window).astype(jnp.float32).astype(jnp.bfloat16)
    usable = lax.dot_general(flags, spread, contract, preferred_element_type=jnp.float32)

    width = 2 * PACK
    for g in range(own // width):
        pieces = [
            spec_ref[g * width // LANES, pl.ds(w, channels, stride=windows), :][
                :, g * width % LANES : g * width % LANES + width
            ]
            for w in range(windows)
        ]
        packed = jnp.concatenate(pieces, axis=1) * usable
        out_ref[:, g * LANES : (g + 1) * LANES] = packed.astype(jnp.bfloat16)


def whiten(strain, channel_ok, window_ok, freq_devices):
    channels, windows, samples = strain.shape
    bin_count = BINS // freq_devices
    tables = jnp.asarray(dft_tables(freq_devices, samples))
    ones = jnp.asarray(smoother(bin_count))
    columns = tables.shape[2]
    own = 2 * bin_count
    rows = channels * windows
    chunks = samples // CHUNK
    return pl.pallas_call(
        whiten_kernel,
        in_specs=[pl.BlockSpec(memory_space=pltpu.HBM)] * 5,
        out_specs=pl.BlockSpec(memory_space=pltpu.VMEM),
        out_shape=pltpu.VMEM((channels, windows * own + LANES), jnp.bfloat16),
        scratch_shapes=[
            pltpu.VMEM((channels, windows, samples), jnp.bfloat16),
            pltpu.VMEM((1, channels), jnp.int32),
            pltpu.VMEM((windows, channels), jnp.int32),
            pltpu.VMEM((samples, columns), jnp.bfloat16),
            pltpu.VMEM((columns, own), jnp.bfloat16),
            pltpu.VMEM((rows, samples + 2 * TIME_HALF), jnp.bfloat16),
            pltpu.VMEM((rows, samples), jnp.bfloat16),
            pltpu.VMEM((-(-own // LANES), rows, LANES), jnp.float32),
            pltpu.SemaphoreType.DMA((chunks,)),
            pltpu.SemaphoreType.DMA((chunks,)),
            pltpu.SemaphoreType.DMA((3,)),
        ],
        compiler_params=pltpu.CompilerParams(vmem_limit_bytes=VMEM_BYTES),
        name="whiten",
    )(
        *(
            pltpu.with_memory_space_constraint(value, pltpu.HBM)
            for value in (strain, channel_ok.reshape(1, channels), window_ok.T, tables, ones)
        )
    )


def trade(value, partner):
    count = lax.axis_size("ch")
    pairs = [(i, partner(i)) for i in range(count) if 0 <= partner(i) < count]
    return lax.ppermute(value, "ch", pairs)


def beside(i):
    return i ^ 1


def partner_pair(i):
    return i ^ 2


def other_pair(i):
    return i + 2 if i // 2 % 2 else i - 2


def partner_far(i):
    return i ^ 4


def other_far(i):
    return i + 4 if i // 4 % 2 else i - 4


def cross_kernel(order, own_ref, mate_ref, *refs):
    arrived = [refs[at + order.index(k)] for at in (0, 4) for k in range(4)]
    (ahead_hbm, behind_hbm, partners_ref, div_ahead, div_behind, *products) = refs[8:-3]
    ahead_ref, behind_ref, sems = refs[-3:]
    channels = own_ref.shape[0]
    packs = own_ref.shape[1] // LANES - 1
    index = lax.axis_index("ch")
    first = lax.rem(index, 2) == 0
    pair = index // 2
    near_up = lax.rem(pair, 2) == 0
    far_up = lax.rem(pair // 2, 2) == 0

    def neighbours(lanes):
        pick = lambda a, b: jnp.where(first, a, b)
        own, mate = own_ref[:, lanes], mate_ref[:, lanes]
        mine, theirs = [r[:, lanes] for r in arrived[:4]], [r[:, lanes] for r in arrived[4:]]
        met = [(pick(a, b), pick(b, a)) for a, b in zip(mine, theirs, strict=True)]
        choose = lambda up, a, b: tuple(jnp.where(up, x, y) for x, y in zip(a, b, strict=True))
        up1, down1 = choose(near_up, met[0], met[1]), choose(near_up, met[1], met[0])
        up2, down2 = choose(far_up, met[2], met[3]), choose(far_up, met[3], met[2])
        ahead = [own, pick(mate, up1[0]), pick(up1[0], up1[1]), pick(up1[1], up2[0]), pick(up2[0], up2[1])]
        behind = [pick(down2[0], down2[1]), pick(down2[1], down1[0]), pick(down1[0], down1[1]), pick(down1[1], mate), own]
        return jnp.concatenate(ahead, axis=0), jnp.concatenate(behind, axis=0)

    total = REACH + channels
    fold = lax.broadcasted_iota(jnp.int32, (total, total), 0)
    source = lax.broadcasted_iota(jnp.int32, (total, total), 1)
    lead = 2 * channels - 1
    wanted = jnp.where(
        fold < channels,
        lead - fold,
        jnp.where(fold < REACH, REACH + lead - fold, REACH + channels - 1 - fold),
    )
    turn = (wanted == source).astype(jnp.float32).astype(jnp.bfloat16)

    def arrange(lanes):
        rows_ahead, rows_behind = neighbours(lanes)
        turned = jnp.dot(turn, rows_behind, preferred_element_type=jnp.float32).astype(jnp.bfloat16)
        partners_ref[:REACH, lanes] = rows_ahead[:REACH]
        partners_ref[REACH : 2 * REACH, lanes] = turned[:REACH]
        partners_ref[2 * REACH : 2 * REACH + channels, lanes] = rows_ahead[REACH:]
        partners_ref[2 * REACH + channels :, lanes] = turned[REACH:]

    row = lax.broadcasted_iota(jnp.int32, (channels, LANES), 0)
    lane = lax.broadcasted_iota(jnp.int32, (channels, LANES), 1)
    wrap_ahead = lane <= row
    wrap_behind = (lane >= channels) & (lane <= lead - row)
    flip = 7 - lax.broadcasted_iota(jnp.int32, (8, LANES), 0)
    part = lax.rem(lane // PACK, 2)

    def turned_rows(v):
        return jnp.take_along_axis(v, flip, axis=0)

    def skewed(ahead, behind, ends):
        a = jnp.where(wrap_ahead, ends, ahead)
        b = jnp.where(wrap_behind, ends, behind)
        aheads = []
        for r in range(0, channels, 8):
            v = pltpu.roll(turned_rows(a[r : r + 8]), (2 * LANES - r - 8) % LANES, 1, stride=1, stride_axis=0)
            aheads.append(turned_rows(v))
        b = pltpu.roll(b, LANES - 2 * channels, 1, stride=1, stride_axis=0)
        return jnp.concatenate(aheads, axis=0), b

    contract = (((1,), (1,)), ((), ()))

    def multiply(g):
        lanes = slice(g * LANES, (g + 1) * LANES)
        a = own_ref[:, lanes].astype(jnp.float32)
        rotated = jnp.where(part == 0, -pltpu.roll(a, LANES - PACK, 1), pltpu.roll(a, PACK, 1))
        zero = jnp.zeros_like(a)
        rows = []
        for f in range(PACK):
            mask = lax.rem(lane, PACK) == f
            rows += [jnp.where(mask, a, zero), jnp.where(mask, rotated, zero)]
        lhs = jnp.concatenate(rows, axis=0).astype(jnp.bfloat16)
        products[g % len(products)][:, : 2 * (REACH + channels)] = lax.dot_general(
            lhs, partners_ref[:, lanes], contract, preferred_element_type=jnp.float32
        )

    def copies(g):
        bins = pl.ds(g * PACK, PACK)
        return [
            pltpu.make_async_copy(held.at[:, bins], out.at[:, bins], sems.at[k, g])
            for k, (held, out) in enumerate(((ahead_ref, ahead_hbm), (behind_ref, behind_hbm)))
        ]

    def finish(g):
        product = products[g % len(products)]
        for f in range(PACK):
            for v in range(2):
                rows = pl.ds((2 * f + v) * channels, channels)
                ahead, behind = skewed(*(product[rows, pl.ds(t * LANES, LANES)] for t in range(3)))
                ahead_ref[v, g * PACK + f] = (ahead * div_ahead[...]).astype(jnp.bfloat16)
                behind_ref[v, g * PACK + f] = (behind * div_behind[...]).astype(jnp.bfloat16)
        for copy in copies(g):
            copy.start()

    flags = slice(packs * LANES, (packs + 1) * LANES)
    for at in range(0, packs * LANES, WIDE):
        arrange(slice(at, min(at + WIDE, packs * LANES)))
    arrange(flags)
    counts = lax.dot_general(
        own_ref[:, flags], partners_ref[:, flags], contract, preferred_element_type=jnp.float32
    )
    products[0][:channels, : 2 * (REACH + channels)] = counts
    ahead, behind = skewed(*(products[0][:channels, t * LANES : (t + 1) * LANES] for t in range(3)))
    div_ahead[...] = 1.0 / jnp.maximum(ahead, 1.0)
    div_behind[...] = 1.0 / jnp.maximum(behind, 1.0)

    for g in range(packs):
        if g == 0:
            multiply(0)
            multiply(1)
        if g + 2 < packs:
            multiply(g + 2)
        finish(g)
    for g in range(packs):
        for copy in copies(g):
            copy.wait()


def cross(values, bin_count, order):
    channels = values[0].shape[0]
    shape = jax.ShapeDtypeStruct((2, bin_count, channels, REACH), jnp.bfloat16)
    products = pltpu.VMEM((2 * PACK * channels, 3 * LANES), jnp.float32)
    held = pltpu.VMEM((2, bin_count, channels, REACH), jnp.bfloat16)
    return pl.pallas_call(
        functools.partial(cross_kernel, order),
        in_specs=[pl.BlockSpec(memory_space=pltpu.VMEM)] * len(values),
        out_specs=[pl.BlockSpec(memory_space=pl.ANY)] * 2,
        out_shape=[shape, shape],
        scratch_shapes=[
            pltpu.VMEM((2 * (REACH + channels), values[0].shape[1]), jnp.bfloat16),
            pltpu.VMEM((channels, REACH), jnp.float32),
            pltpu.VMEM((channels, REACH), jnp.float32),
            products,
            products,
            products,
            held,
            held,
            pltpu.SemaphoreType.DMA((2, bin_count // PACK)),
        ],
        compiler_params=pltpu.CompilerParams(vmem_limit_bytes=VMEM_BYTES),
        name="cross",
    )(*values)


def per_device(strain, channel_ok, window_ok):
    freq_devices = lax.axis_size("freq")
    own = whiten(strain, channel_ok, window_ok, freq_devices)
    mate = trade(own, beside)
    arrived = [trade(own, f) for f in (partner_pair, other_pair, partner_far, other_far)]
    shared = [trade(block, beside) for block in arrived]
    order = (3, 2, 0, 1)
    last = [arrived[k] for k in order] + [shared[k] for k in order]
    return cross([own, mate, *last], BINS // freq_devices, order)


def solution(mesh):
    return jax.shard_map(
        per_device,
        mesh=mesh,
        in_specs=(P("ch", None, None), P("ch"), P("ch", None)),
        out_specs=(P(None, "freq", "ch", None), P(None, "freq", "ch", None)),
        check_vma=False,
    )
```

time: 36 us -> 22.5 us (0.62)
  the two profiles are of different devices: /device:TPU:17 before, /device:TPU:0 now
where the time goes in v2:
time: 22.5 us; the launch traced here: 22.4 us
  starting transfers between devices  9.78 us (43%)
  Pallas kernels  7.48 us (33%)
  waiting for transfers between devices  4.43 us (20%)
  between operations  0.68 us (3%)
    ppermute x9, starting transfers between devices, trade(): return lax.ppermute(value, 'ch', pairs)  9.78 us
    ppermute x9, waiting for transfers between devices, trade(): return lax.ppermute(value, 'ch', pairs)  4.43 us
    pallas_call x1, Pallas kernels, cross(): pl.pallas_call(functools.partial(cross_kernel, order), in_specs=[pl.Block...  3.79 us
    pallas_call x1, Pallas kernels, whiten(): pl.pallas_call(whiten_kernel, in_specs=[pl.BlockSpec(memory_space=pltpu.H...  3.69 us
  transfers between devices with their start and end apart: 9, of which 4 were waited for; matrix products, arithmetic and copies ran while one was open for 0% of the time, Pallas kernels for 0%

profile of v2, /device:TPU:0, one launch (start us, length us, event | category | flops | bytes accessed | tf_op | source)
XLA Modules:
  0.0 22.4 jit_solution(11564147385953570499)
XLA Ops:
  0.6 3.7 %whiten.1.own_ref = bf16[32,2176]{1,0:T(8,128)(2,1)S(1)} custom-call(bf16[32,8,2048]{2,1,0:T(8,128)(2,1)} %x_hbm.1, s32[1,32]{1,0:T(1,128)} %bitcast.3, s32[8,32]{1,0:T(8,128)} %bitcast.2, bf16[2,2048,384]{2,1,0:T(8,128)(2,1)} %constant.4.clone.table_hbm, bf16[384,256]{1,0:T(8,128)(2,1)} %constant.5.clone.smooth_hbm), custom_call_target="tpu_custom_call" | custom-call | tf_op jit(solution)/shard_map/whiten/pallas_call | solution.py:162
  4.3 0.7 %collective-permute-start.4 = (bf16[32,2176]{1,0:T(8,128)(2,1)S(1)}, bf16[32,2176]{1,0:T(8,128)(2,1)S(1)}, u32[]{:S(2)}, u32[]{:S(2)}) collective-permute-start(bf16[32,2176]{1,0:T(8,128)(2,1)S(1)} %whiten.1.own_ref), channel_id=1, source_target_pairs={{4,8},{6,10},{8,4},{10,6},{12,16},{14,18},{16,12},{18,14},{20,24},... | collective-permute-start | bytes 417800 | tf_op jit(solution)/shard_map/ppermute | solution.py:193
  5.0 5.8 %collective-permute-start.3 = (bf16[32,2176]{1,0:T(8,128)(2,1)S(1)}, bf16[32,2176]{1,0:T(8,128)(2,1)S(1)}, u32[]{:S(2)}, u32[]{:S(2)}) collective-permute-start(bf16[32,2176]{1,0:T(8,128)(2,1)S(1)} %whiten.1.own_ref), channel_id=1, source_target_pairs={{0,4},{2,6},{4,0},{6,2},{8,12},{10,14},{12,8},{14,10},{16,20},{18,... | collective-permute-start | bytes 417800 | tf_op jit(solution)/shard_map/ppermute | solution.py:193
  10.8 1.6 %collective-permute-start.2 = (bf16[32,2176]{1,0:T(8,128)(2,1)S(1)}, bf16[32,2176]{1,0:T(8,128)(2,1)S(1)}, u32[]{:S(2)}, u32[]{:S(2)}) collective-permute-start(bf16[32,2176]{1,0:T(8,128)(2,1)S(1)} %whiten.1.own_ref), channel_id=1, source_target_pairs={{0,8},{2,10},{4,12},{6,14},{8,0},{10,2},{12,4},{14,6},{16,24},{18,... | collective-permute-start | bytes 417800 | tf_op jit(solution)/shard_map/ppermute | solution.py:193
  12.4 0.7 %collective-permute-start.1 = (bf16[32,2176]{1,0:T(8,128)(2,1)S(1)}, bf16[32,2176]{1,0:T(8,128)(2,1)S(1)}, u32[]{:S(2)}, u32[]{:S(2)}) collective-permute-start(bf16[32,2176]{1,0:T(8,128)(2,1)S(1)} %whiten.1.own_ref), channel_id=1, source_target_pairs={{8,16},{10,18},{12,20},{14,22},{16,8},{18,10},{20,12},{22,14},{9,1... | collective-permute-start | bytes 417800 | tf_op jit(solution)/shard_map/ppermute | solution.py:193
  13.0 0.1 collective-permute-start
  13.1 0.0 collective-permute-done.4.refs_3_
  13.1 0.5 %collective-permute-start.8 = (bf16[32,2176]{1,0:T(8,128)(2,1)S(1)}, bf16[32,2176]{1,0:T(8,128)(2,1)S(1)}, u32[]{:S(2)}, u32[]{:S(2)}) collective-permute-start(bf16[32,2176]{1,0:T(8,128)(2,1)S(1)} %collective-permute-done.4.refs_3_), channel_id=1, source_target_pairs={{0,2},{2,0},{4,6},{6,4},{8,10},{10,8},{12,14},{14,12},{16,18},{18,... | collective-permute-start | bytes 417800 | tf_op jit(solution)/shard_map/ppermute | solution.py:193
  13.6 2.4 %collective-permute-done.3.refs_2_ = bf16[32,2176]{1,0:T(8,128)(2,1)S(1)} collective-permute-done((bf16[32,2176]{1,0:T(8,128)(2,1)S(1)}, bf16[32,2176]{1,0:T(8,128)(2,1)S(1)}, u32[]{:S(2)}, u32[]{:S(2)}) %collective-permute-start.3) | collective-permute-done | bytes 139296 | tf_op jit(solution)/shard_map/ppermute | solution.py:193
  16.0 0.0 collective-permute-start.7
  16.0 1.0 %collective-permute-done.2.refs_1_ = bf16[32,2176]{1,0:T(8,128)(2,1)S(1)} collective-permute-done((bf16[32,2176]{1,0:T(8,128)(2,1)S(1)}, bf16[32,2176]{1,0:T(8,128)(2,1)S(1)}, u32[]{:S(2)}, u32[]{:S(2)}) %collective-permute-start.2) | collective-permute-done | bytes 139296 | tf_op jit(solution)/shard_map/ppermute | solution.py:193
  17.0 0.0 collective-permute-start.6
  17.0 0.0 collective-permute-done.1.refs_0_
  17.0 0.5 %collective-permute-start.5 = (bf16[32,2176]{1,0:T(8,128)(2,1)S(1)}, bf16[32,2176]{1,0:T(8,128)(2,1)S(1)}, u32[]{:S(2)}, u32[]{:S(2)}) collective-permute-start(bf16[32,2176]{1,0:T(8,128)(2,1)S(1)} %collective-permute-done.1.refs_0_), channel_id=1, source_target_pairs={{0,2},{2,0},{4,6},{6,4},{8,10},{10,8},{12,14},{14,12},{16,18},{18,... | collective-permute-start | bytes 417800 | tf_op jit(solution)/shard_map/ppermute | solution.py:193
  17.5 0.0 collective-permute-done.mate_ref
  17.5 0.0 collective-permute-done.8.refs_7_
  17.5 0.0 collective-permute-done.7.refs_6_
  17.5 0.8 %collective-permute-done.6.refs_5_ = bf16[32,2176]{1,0:T(8,128)(2,1)S(1)} collective-permute-done((bf16[32,2176]{1,0:T(8,128)(2,1)S(1)}, bf16[32,2176]{1,0:T(8,128)(2,1)S(1)}, u32[]{:S(2)}, u32[]{:S(2)}) %collective-permute-start.6) | collective-permute-done | bytes 139296 | tf_op jit(solution)/shard_map/ppermute | solution.py:193
  18.4 0.2 collective-permute-done.5.refs_4_
  18.6 3.8 %cross.1 = (bf16[2,128,32,128]{3,2,1,0:T(8,128)(2,1)}, bf16[2,128,32,128]{3,2,1,0:T(8,128)(2,1)}) custom-call(bf16[32,2176]{1,0:T(8,128)(2,1)S(1)} %whiten.1.own_ref, bf16[32,2176]{1,0:T(8,128)(2,1)S(1)} %collective-permute-done.mate_ref, bf16[32,2176]{1,0:T(8,128)(2,1)S(1)} %collective-permute-done.1.refs_0_, ...), custom_call_target="tpu_custom_call" | custom-call | tf_op jit(solution)/shard_map/cross/pallas_call | solution.py:342
Async XLA Ops:
  4.3 8.8 %collective-permute-start.4 = (bf16[32,2176]{1,0:T(8,128)(2,1)S(1)}, bf16[32,2176]{1,0:T(8,128)(2,1)S(1)}, u32[]{:S(2)}, u32[]{:S(2)}) collective-permute-start(bf16[32,2176]{1,0:T(8,128)(2,1)S(1)} %whiten.1.own_ref), channel_id=1, source_target_pairs={{4,8},{6,10},{8,4},{10,6},{12,16},{14,18},{16,12},{18,14},{20,24},... | collective-permute-start | bytes 417800 | tf_op jit(solution)/shard_map/ppermute | solution.py:193
  5.0 11.0 %collective-permute-start.3 = (bf16[32,2176]{1,0:T(8,128)(2,1)S(1)}, bf16[32,2176]{1,0:T(8,128)(2,1)S(1)}, u32[]{:S(2)}, u32[]{:S(2)}) collective-permute-start(bf16[32,2176]{1,0:T(8,128)(2,1)S(1)} %whiten.1.own_ref), channel_id=1, source_target_pairs={{0,4},{2,6},{4,0},{6,2},{8,12},{10,14},{12,8},{14,10},{16,20},{18,... | collective-permute-start | bytes 417800 | tf_op jit(solution)/shard_map/ppermute | solution.py:193
  10.8 6.2 %collective-permute-start.2 = (bf16[32,2176]{1,0:T(8,128)(2,1)S(1)}, bf16[32,2176]{1,0:T(8,128)(2,1)S(1)}, u32[]{:S(2)}, u32[]{:S(2)}) collective-permute-start(bf16[32,2176]{1,0:T(8,128)(2,1)S(1)} %whiten.1.own_ref), channel_id=1, source_target_pairs={{0,8},{2,10},{4,12},{6,14},{8,0},{10,2},{12,4},{14,6},{16,24},{18,... | collective-permute-start | bytes 417800 | tf_op jit(solution)/shard_map/ppermute | solution.py:193
  12.4 4.7 %collective-permute-start.1 = (bf16[32,2176]{1,0:T(8,128)(2,1)S(1)}, bf16[32,2176]{1,0:T(8,128)(2,1)S(1)}, u32[]{:S(2)}, u32[]{:S(2)}) collective-permute-start(bf16[32,2176]{1,0:T(8,128)(2,1)S(1)} %whiten.1.own_ref), channel_id=1, source_target_pairs={{8,16},{10,18},{12,20},{14,22},{16,8},{18,10},{20,12},{22,14},{9,1... | collective-permute-start | bytes 417800 | tf_op jit(solution)/shard_map/ppermute | solution.py:193
  13.0 4.5 %collective-permute-start = (bf16[32,2176]{1,0:T(8,128)(2,1)S(1)}, bf16[32,2176]{1,0:T(8,128)(2,1)S(1)}, u32[]{:S(2)}, u32[]{:S(2)}) collective-permute-start(bf16[32,2176]{1,0:T(8,128)(2,1)S(1)} %whiten.1.own_ref), channel_id=1, source_target_pairs={{0,2},{2,0},{4,6},{6,4},{8,10},{10,8},{12,14},{14,12},{16,18},{18,... | collective-permute-start | bytes 417800 | tf_op jit(solution)/shard_map/ppermute | solution.py:193
  13.1 4.4 %collective-permute-start.8 = (bf16[32,2176]{1,0:T(8,128)(2,1)S(1)}, bf16[32,2176]{1,0:T(8,128)(2,1)S(1)}, u32[]{:S(2)}, u32[]{:S(2)}) collective-permute-start(bf16[32,2176]{1,0:T(8,128)(2,1)S(1)} %collective-permute-done.4.refs_3_), channel_id=1, source_target_pairs={{0,2},{2,0},{4,6},{6,4},{8,10},{10,8},{12,14},{14,12},{16,18},{18,... | collective-permute-start | bytes 417800 | tf_op jit(solution)/shard_map/ppermute | solution.py:193
  16.0 1.5 %collective-permute-start.7 = (bf16[32,2176]{1,0:T(8,128)(2,1)S(1)}, bf16[32,2176]{1,0:T(8,128)(2,1)S(1)}, u32[]{:S(2)}, u32[]{:S(2)}) collective-permute-start(bf16[32,2176]{1,0:T(8,128)(2,1)S(1)} %collective-permute-done.3.refs_2_), channel_id=1, source_target_pairs={{0,2},{2,0},{4,6},{6,4},{8,10},{10,8},{12,14},{14,12},{16,18},{18,... | collective-permute-start | bytes 417800 | tf_op jit(solution)/shard_map/ppermute | solution.py:193
  17.0 1.4 %collective-permute-start.6 = (bf16[32,2176]{1,0:T(8,128)(2,1)S(1)}, bf16[32,2176]{1,0:T(8,128)(2,1)S(1)}, u32[]{:S(2)}, u32[]{:S(2)}) collective-permute-start(bf16[32,2176]{1,0:T(8,128)(2,1)S(1)} %collective-permute-done.2.refs_1_), channel_id=1, source_target_pairs={{0,2},{2,0},{4,6},{6,4},{8,10},{10,8},{12,14},{14,12},{16,18},{18,... | collective-permute-start | bytes 417800 | tf_op jit(solution)/shard_map/ppermute | solution.py:193
  17.0 1.6 %collective-permute-start.5 = (bf16[32,2176]{1,0:T(8,128)(2,1)S(1)}, bf16[32,2176]{1,0:T(8,128)(2,1)S(1)}, u32[]{:S(2)}, u32[]{:S(2)}) collective-permute-start(bf16[32,2176]{1,0:T(8,128)(2,1)S(1)} %collective-permute-done.1.refs_0_), channel_id=1, source_target_pairs={{0,2},{2,0},{4,6},{6,4},{8,10},{10,8},{12,14},{14,12},{16,18},{18,... | collective-permute-start | bytes 417800 | tf_op jit(solution)/shard_map/ppermute | solution.py:193

commit v3 on v2

--- a/solution.py
+++ b/solution.py
@@ -17,6 +17,7 @@
 BIN_HALF = 32
 LANES = 128
 PACK = LANES // (2 * WINDOWS)
+HALVES = 1
 CHUNK = 2048
 WIDE = 512
 VMEM_BYTES = 40 * 1024 * 1024
@@ -113,20 +114,6 @@
         ).astype(jnp.bfloat16)
     for copy in table_copies + small_copies:
         copy.wait()
-    spectra = jnp.dot(level_ref[...], table_ref[...], preferred_element_type=jnp.float32)
-
-    power = spectra * spectra
-    high = power.astype(jnp.bfloat16)
-    low = (power - high.astype(jnp.float32)).astype(jnp.bfloat16)
-    ones = smooth_ref[...]
-    smooth = jnp.dot(high, ones, preferred_element_type=jnp.float32) + jnp.dot(
-        low, ones, preferred_element_type=jnp.float32
-    )
-    white = spectra[:, halo:] * lax.rsqrt(smooth * (1.0 / (2 * BIN_HALF + 1)) + 1e-06)
-    for t in range(0, own, LANES):
-        width = min(LANES, own - t)
-        spec_ref[t // LANES, :, :width] = white[:, t : t + width]
-
     flags = (ok_ref[...] * win_ref[...]).astype(jnp.float32).astype(jnp.bfloat16)
     lane = lax.broadcasted_iota(jnp.int32, (windows, LANES), 1)
     window = lax.broadcasted_iota(jnp.int32, (windows, LANES), 0)
@@ -135,19 +122,45 @@
     out_ref[:, windows * own :] = lax.dot_general(
         flags, picked, contract, preferred_element_type=jnp.float32
     ).astype(jnp.bfloat16)
-    spread = (lane // (2 * PACK) == window).astype(jnp.float32).astype(jnp.bfloat16)
-    usable = lax.dot_general(flags, spread, contract, preferred_element_type=jnp.float32)
-
     width = 2 * PACK
-    for g in range(own // width):
-        pieces = [
-            spec_ref[g * width // LANES, pl.ds(w, channels, stride=windows), :][
-                :, g * width % LANES : g * width % LANES + width
-            ]
-            for w in range(windows)
-        ]
-        packed = jnp.concatenate(pieces, axis=1) * usable
-        out_ref[:, g * LANES : (g + 1) * LANES] = packed.astype(jnp.bfloat16)
+    usable = []
+    for g in range(LANES // width):
+        spread = (lax.rem(lane // width + windows - g, windows) == window).astype(jnp.float32)
+        usable.append(
+            lax.dot_general(
+                flags, spread.astype(jnp.bfloat16), contract, preferred_element_type=jnp.float32
+            )
+        )
+
+    ones = smooth_ref[...]
+    half = channels // HALVES
+    block = lax.broadcasted_iota(jnp.int32, (half, LANES), 1) // width
+    for h in range(HALVES):
+        part = slice(h * half * windows, (h + 1) * half * windows)
+        spectra = jnp.dot(level_ref[part], table_ref[...], preferred_element_type=jnp.float32)
+        power = spectra * spectra
+        high = power.astype(jnp.bfloat16)
+        low = (power - high.astype(jnp.float32)).astype(jnp.bfloat16)
+        smooth = jnp.dot(high, ones, preferred_element_type=jnp.float32) + jnp.dot(
+            low, ones, preferred_element_type=jnp.float32
+        )
+        white = spectra[:, halo:] * lax.rsqrt(smooth * (1.0 / (2 * BIN_HALF + 1)) + 1e-06)
+        for t in range(0, own, LANES):
+            tile_width = min(LANES, own - t)
+            tile_white = white[:, t : t + tile_width]
+            if tile_width < LANES:
+                rest = jnp.zeros((half * windows, LANES - tile_width), jnp.float32)
+                tile_white = jnp.concatenate([tile_white, rest], axis=1)
+            turned = pltpu.roll(tile_white, 0, 1, stride=width, stride_axis=0)
+            spec_ref[h, t // LANES] = turned
+            windows_of = [spec_ref[h, t // LANES, pl.ds(w, half, stride=windows), :] for w in range(windows)]
+            for g in range(tile_width // width):
+                packed = windows_of[0]
+                for w in range(1, windows):
+                    packed = jnp.where(block == (g + w) % windows, windows_of[w], packed)
+                packed = packed * usable[g][h * half : (h + 1) * half]
+                at = (t // width + g) * LANES
+                out_ref[h * half : (h + 1) * half, at : at + LANES] = packed.astype(jnp.bfloat16)
 
 
 def whiten(strain, channel_ok, window_ok, freq_devices):
@@ -172,7 +185,7 @@
             pltpu.VMEM((columns, own), jnp.bfloat16),
             pltpu.VMEM((rows, samples + 2 * TIME_HALF), jnp.bfloat16),
             pltpu.VMEM((rows, samples), jnp.bfloat16),
-            pltpu.VMEM((-(-own // LANES), rows, LANES), jnp.float32),
+            pltpu.VMEM((HALVES, -(-own // LANES), rows // HALVES, LANES), jnp.float32),
             pltpu.SemaphoreType.DMA((chunks,)),
             pltpu.SemaphoreType.DMA((chunks,)),
             pltpu.SemaphoreType.DMA((3,)),
@@ -189,33 +202,36 @@
 
 def trade(value, partner):
     count = lax.axis_size("ch")
-    pairs = [(i, partner(i)) for i in range(count) if 0 <= partner(i) < count]
-    return lax.ppermute(value, "ch", pairs)
+    inside = lambda i: 0 <= partner(i) < count
+    return lax.ppermute(value, "ch", [(i, partner(i) if inside(i) else beside(i)) for i in range(count)])
 
 
 def beside(i):
-    return i ^ 1
+    return i + 1 - 2 * (i % 2)
 
 
 def partner_pair(i):
-    return i ^ 2
+    return i + 2 - 4 * (i // 2 % 2)
 
 
 def other_pair(i):
-    return i + 2 if i // 2 % 2 else i - 2
+    return i - 2 + 4 * (i // 2 % 2)
 
 
 def partner_far(i):
-    return i ^ 4
+    return i + 4 - 8 * (i // 4 % 2)
 
 
 def other_far(i):
-    return i + 4 if i // 4 % 2 else i - 4
+    return i - 4 + 8 * (i // 4 % 2)
+
+
+TRADES = (partner_pair, other_pair, partner_far, other_far)
 
 
 def cross_kernel(order, own_ref, mate_ref, *refs):
     arrived = [refs[at + order.index(k)] for at in (0, 4) for k in range(4)]
-    (ahead_hbm, behind_hbm, partners_ref, div_ahead, div_behind, *products) = refs[8:-3]
+    (ahead_hbm, behind_hbm, partners_ref, div_ahead, div_behind, count_ref, *products) = refs[8:-3]
     ahead_ref, behind_ref, sems = refs[-3:]
     channels = own_ref.shape[0]
     packs = own_ref.shape[1] // LANES - 1
@@ -224,12 +240,16 @@
     pair = index // 2
     near_up = lax.rem(pair, 2) == 0
     far_up = lax.rem(pair // 2, 2) == 0
+    count = lax.axis_size("ch")
+    met_index = [partner(index) for partner in TRADES]
+    inside = [(i >= 0) & (i < count) for i in met_index]
 
     def neighbours(lanes):
         pick = lambda a, b: jnp.where(first, a, b)
         own, mate = own_ref[:, lanes], mate_ref[:, lanes]
         mine, theirs = [r[:, lanes] for r in arrived[:4]], [r[:, lanes] for r in arrived[4:]]
         met = [(pick(a, b), pick(b, a)) for a, b in zip(mine, theirs, strict=True)]
+        met = [tuple(jnp.where(ok, x, jnp.zeros_like(x)) for x in blocks) for ok, blocks in zip(inside, met, strict=True)]
         choose = lambda up, a, b: tuple(jnp.where(up, x, y) for x, y in zip(a, b, strict=True))
         up1, down1 = choose(near_up, met[0], met[1]), choose(near_up, met[1], met[0])
         up2, down2 = choose(far_up, met[2], met[3]), choose(far_up, met[3], met[2])
@@ -311,21 +331,22 @@
             copy.start()
 
     flags = slice(packs * LANES, (packs + 1) * LANES)
-    for at in range(0, packs * LANES, WIDE):
-        arrange(slice(at, min(at + WIDE, packs * LANES)))
-    arrange(flags)
-    counts = lax.dot_general(
-        own_ref[:, flags], partners_ref[:, flags], contract, preferred_element_type=jnp.float32
-    )
-    products[0][:channels, : 2 * (REACH + channels)] = counts
-    ahead, behind = skewed(*(products[0][:channels, t * LANES : (t + 1) * LANES] for t in range(3)))
-    div_ahead[...] = 1.0 / jnp.maximum(ahead, 1.0)
-    div_behind[...] = 1.0 / jnp.maximum(behind, 1.0)
-
+    lead_packs = WIDE // LANES
     for g in range(packs):
         if g == 0:
+            arrange(flags)
+            count_ref[:, : 2 * (REACH + channels)] = lax.dot_general(
+                own_ref[:, flags], partners_ref[:, flags], contract, preferred_element_type=jnp.float32
+            )
+            arrange(slice(0, WIDE))
             multiply(0)
             multiply(1)
+            ahead, behind = skewed(*(count_ref[:, t * LANES : (t + 1) * LANES] for t in range(3)))
+            div_ahead[...] = 1.0 / jnp.maximum(ahead, 1.0)
+            div_behind[...] = 1.0 / jnp.maximum(behind, 1.0)
+        at = g + lead_packs
+        if at < packs and at % lead_packs == 0:
+            arrange(slice(at * LANES, (at + lead_packs) * LANES))
         if g + 2 < packs:
             multiply(g + 2)
         finish(g)
@@ -348,6 +369,7 @@
             pltpu.VMEM((2 * (REACH + channels), values[0].shape[1]), jnp.bfloat16),
             pltpu.VMEM((channels, REACH), jnp.float32),
             pltpu.VMEM((channels, REACH), jnp.float32),
+            pltpu.VMEM((channels, 3 * LANES), jnp.float32),
             products,
             products,
             products,
@@ -364,9 +386,9 @@
     freq_devices = lax.axis_size("freq")
     own = whiten(strain, channel_ok, window_ok, freq_devices)
     mate = trade(own, beside)
-    arrived = [trade(own, f) for f in (partner_pair, other_pair, partner_far, other_far)]
+    arrived = [trade(own, partner) for partner in TRADES]
     shared = [trade(block, beside) for block in arrived]
-    order = (3, 2, 0, 1)
+    order = (2, 3, 0, 1)
     last = [arrived[k] for k in order] + [shared[k] for k in order]
     return cross([own, mate, *last], BINS // freq_devices, order)
 

time: 22.5 us -> 20.2 us (0.90)
  starting transfers between devices: 9.78 us -> 8.73 us
  waiting for transfers between devices: 4.43 us -> 3.53 us
  Pallas kernels: 7.48 us -> 7.16 us
    ppermute x9, starting transfers between devices: 9.78 us -> 8.73 us  [trade(): lax.ppermute(value, 'ch', [(i, partner(i) if inside(i) else beside(i)) fo...]
    ppermute x9, waiting for transfers between devices: 4.43 us -> 3.53 us  [trade(): lax.ppermute(value, 'ch', [(i, partner(i) if inside(i) else beside(i)) fo...]
    pallas_call x1, Pallas kernels: 3.69 us -> 3.41 us  [whiten(): pl.pallas_call(whiten_kernel, in_specs=[pl.BlockSpec(memory_space=pltpu.H...]
  transfers between devices with their start and end apart: 9 -> 9, of which waited for: 4 -> 5; matrix products, arithmetic and copies ran while one was open for 0% -> 0% of each run, Pallas kernels for 0% -> 0%
where the time goes in v3:
time: 20.2 us; the launch traced here: 20.1 us
  starting transfers between devices  8.73 us (43%)
  Pallas kernels  7.16 us (35%)
  waiting for transfers between devices  3.53 us (17%)
  between operations  0.65 us (3%)
    ppermute x9, starting transfers between devices, trade(): lax.ppermute(value, 'ch', [(i, partner(i) if inside(i) else beside(i)) fo...  8.73 us
    pallas_call x1, Pallas kernels, cross(): pl.pallas_call(functools.partial(cross_kernel, order), in_specs=[pl.Block...  3.74 us
    ppermute x9, waiting for transfers between devices, trade(): lax.ppermute(value, 'ch', [(i, partner(i) if inside(i) else beside(i)) fo...  3.53 us
    pallas_call x1, Pallas kernels, whiten(): pl.pallas_call(whiten_kernel, in_specs=[pl.BlockSpec(memory_space=pltpu.H...  3.41 us
  transfers between devices with their start and end apart: 9, of which 5 were waited for; matrix products, arithmetic and copies ran while one was open for 0% of the time, Pallas kernels for 0%

profile of v3, /device:TPU:0, one launch (start us, length us, event | category | flops | bytes accessed | tf_op | source)
XLA Modules:
  0.0 20.1 jit_solution(11651873475608368974)
XLA Ops:
  0.6 3.4 %whiten.1.own_ref = bf16[32,2176]{1,0:T(8,128)(2,1)S(1)} custom-call(bf16[32,8,2048]{2,1,0:T(8,128)(2,1)} %x_hbm.1, s32[1,32]{1,0:T(1,128)} %bitcast.3, s32[8,32]{1,0:T(8,128)} %bitcast.2, bf16[2,2048,384]{2,1,0:T(8,128)(2,1)} %constant.4.clone.table_hbm, bf16[384,256]{1,0:T(8,128)(2,1)} %constant.5.clone.smooth_hbm), custom_call_target="tpu_custom_call" | custom-call | tf_op jit(solution)/shard_map/whiten/pallas_call | solution.py:175
  4.0 0.5 %collective-permute-start.4 = (bf16[32,2176]{1,0:T(8,128)(2,1)S(1)}, bf16[32,2176]{1,0:T(8,128)(2,1)S(1)}, u32[]{:S(2)}, u32[]{:S(2)}) collective-permute-start(bf16[32,2176]{1,0:T(8,128)(2,1)S(1)} %whiten.1.own_ref), channel_id=1, source_target_pairs={{0,2},{2,0},{4,8},{6,10},{8,4},{10,6},{12,16},{14,18},{16,12},{18,... | collective-permute-start | bytes 417800 | tf_op jit(solution)/shard_map/ppermute | solution.py:206
  4.6 4.0 %collective-permute-start.3 = (bf16[32,2176]{1,0:T(8,128)(2,1)S(1)}, bf16[32,2176]{1,0:T(8,128)(2,1)S(1)}, u32[]{:S(2)}, u32[]{:S(2)}) collective-permute-start(bf16[32,2176]{1,0:T(8,128)(2,1)S(1)} %whiten.1.own_ref), channel_id=1, source_target_pairs={{0,4},{2,6},{4,0},{6,2},{8,12},{10,14},{12,8},{14,10},{16,20},{18,... | collective-permute-start | bytes 417800 | tf_op jit(solution)/shard_map/ppermute | solution.py:206
  8.6 0.0 collective-permute-start.2
  8.6 3.2 %collective-permute-start.1 = (bf16[32,2176]{1,0:T(8,128)(2,1)S(1)}, bf16[32,2176]{1,0:T(8,128)(2,1)S(1)}, u32[]{:S(2)}, u32[]{:S(2)}) collective-permute-start(bf16[32,2176]{1,0:T(8,128)(2,1)S(1)} %whiten.1.own_ref), channel_id=1, source_target_pairs={{0,8},{2,10},{4,12},{6,14},{8,0},{10,2},{12,4},{14,6},{16,24},{18,... | collective-permute-start | bytes 417800 | tf_op jit(solution)/shard_map/ppermute | solution.py:206
  11.8 0.0 collective-permute-start
  11.8 0.0 collective-permute-done.4.refs_3_
  11.8 0.5 %collective-permute-start.8 = (bf16[32,2176]{1,0:T(8,128)(2,1)S(1)}, bf16[32,2176]{1,0:T(8,128)(2,1)S(1)}, u32[]{:S(2)}, u32[]{:S(2)}) collective-permute-start(bf16[32,2176]{1,0:T(8,128)(2,1)S(1)} %collective-permute-done.4.refs_3_), channel_id=1, source_target_pairs={{0,2},{2,0},{4,6},{6,4},{8,10},{10,8},{12,14},{14,12},{16,18},{18,... | collective-permute-start | bytes 417800 | tf_op jit(solution)/shard_map/ppermute | solution.py:206
  12.3 1.6 %collective-permute-done.3.refs_2_ = bf16[32,2176]{1,0:T(8,128)(2,1)S(1)} collective-permute-done((bf16[32,2176]{1,0:T(8,128)(2,1)S(1)}, bf16[32,2176]{1,0:T(8,128)(2,1)S(1)}, u32[]{:S(2)}, u32[]{:S(2)}) %collective-permute-start.3) | collective-permute-done | bytes 139296 | tf_op jit(solution)/shard_map/ppermute | solution.py:206
  13.9 0.0 collective-permute-start.7
  13.9 0.0 collective-permute-done.2.refs_1_
  13.9 0.5 %collective-permute-start.6 = (bf16[32,2176]{1,0:T(8,128)(2,1)S(1)}, bf16[32,2176]{1,0:T(8,128)(2,1)S(1)}, u32[]{:S(2)}, u32[]{:S(2)}) collective-permute-start(bf16[32,2176]{1,0:T(8,128)(2,1)S(1)} %collective-permute-done.2.refs_1_), channel_id=1, source_target_pairs={{0,2},{2,0},{4,6},{6,4},{8,10},{10,8},{12,14},{14,12},{16,18},{18,... | collective-permute-start | bytes 417800 | tf_op jit(solution)/shard_map/ppermute | solution.py:206
  14.4 0.5 %collective-permute-done.1.refs_0_ = bf16[32,2176]{1,0:T(8,128)(2,1)S(1)} collective-permute-done((bf16[32,2176]{1,0:T(8,128)(2,1)S(1)}, bf16[32,2176]{1,0:T(8,128)(2,1)S(1)}, u32[]{:S(2)}, u32[]{:S(2)}) %collective-permute-start.1) | collective-permute-done | bytes 139296 | tf_op jit(solution)/shard_map/ppermute | solution.py:206
  15.0 0.0 collective-permute-start.5
  15.0 0.0 collective-permute-done.mate_ref
  15.0 0.0 collective-permute-done.8.refs_7_
  15.0 0.3 %collective-permute-done.7.refs_6_ = bf16[32,2176]{1,0:T(8,128)(2,1)S(1)} collective-permute-done((bf16[32,2176]{1,0:T(8,128)(2,1)S(1)}, bf16[32,2176]{1,0:T(8,128)(2,1)S(1)}, u32[]{:S(2)}, u32[]{:S(2)}) %collective-permute-start.7) | collective-permute-done | bytes 139296 | tf_op jit(solution)/shard_map/ppermute | solution.py:206
  15.3 0.2 collective-permute-done.6.refs_5_
  15.5 0.9 %collective-permute-done.5.refs_4_ = bf16[32,2176]{1,0:T(8,128)(2,1)S(1)} collective-permute-done((bf16[32,2176]{1,0:T(8,128)(2,1)S(1)}, bf16[32,2176]{1,0:T(8,128)(2,1)S(1)}, u32[]{:S(2)}, u32[]{:S(2)}) %collective-permute-start.5) | collective-permute-done | bytes 139296 | tf_op jit(solution)/shard_map/ppermute | solution.py:206
  16.3 3.7 %cross.1 = (bf16[2,128,32,128]{3,2,1,0:T(8,128)(2,1)}, bf16[2,128,32,128]{3,2,1,0:T(8,128)(2,1)}) custom-call(bf16[32,2176]{1,0:T(8,128)(2,1)S(1)} %whiten.1.own_ref, bf16[32,2176]{1,0:T(8,128)(2,1)S(1)} %collective-permute-done.mate_ref, bf16[32,2176]{1,0:T(8,128)(2,1)S(1)} %collective-permute-done.1.refs_0_, ...), custom_call_target="tpu_custom_call" | custom-call | tf_op jit(solution)/shard_map/cross/pallas_call | solution.py:363
Async XLA Ops:
  4.0 7.7 %collective-permute-start.4 = (bf16[32,2176]{1,0:T(8,128)(2,1)S(1)}, bf16[32,2176]{1,0:T(8,128)(2,1)S(1)}, u32[]{:S(2)}, u32[]{:S(2)}) collective-permute-start(bf16[32,2176]{1,0:T(8,128)(2,1)S(1)} %whiten.1.own_ref), channel_id=1, source_target_pairs={{0,2},{2,0},{4,8},{6,10},{8,4},{10,6},{12,16},{14,18},{16,12},{18,... | collective-permute-start | bytes 417800 | tf_op jit(solution)/shard_map/ppermute | solution.py:206
  4.6 9.3 %collective-permute-start.3 = (bf16[32,2176]{1,0:T(8,128)(2,1)S(1)}, bf16[32,2176]{1,0:T(8,128)(2,1)S(1)}, u32[]{:S(2)}, u32[]{:S(2)}) collective-permute-start(bf16[32,2176]{1,0:T(8,128)(2,1)S(1)} %whiten.1.own_ref), channel_id=1, source_target_pairs={{0,4},{2,6},{4,0},{6,2},{8,12},{10,14},{12,8},{14,10},{16,20},{18,... | collective-permute-start | bytes 417800 | tf_op jit(solution)/shard_map/ppermute | solution.py:206
  8.6 5.3 %collective-permute-start.2 = (bf16[32,2176]{1,0:T(8,128)(2,1)S(1)}, bf16[32,2176]{1,0:T(8,128)(2,1)S(1)}, u32[]{:S(2)}, u32[]{:S(2)}) collective-permute-start(bf16[32,2176]{1,0:T(8,128)(2,1)S(1)} %whiten.1.own_ref), channel_id=1, source_target_pairs={{0,2},{2,0},{4,6},{6,4},{8,16},{10,18},{12,20},{14,22},{16,8},{18,... | collective-permute-start | bytes 417800 | tf_op jit(solution)/shard_map/ppermute | solution.py:206
  8.6 6.4 %collective-permute-start.1 = (bf16[32,2176]{1,0:T(8,128)(2,1)S(1)}, bf16[32,2176]{1,0:T(8,128)(2,1)S(1)}, u32[]{:S(2)}, u32[]{:S(2)}) collective-permute-start(bf16[32,2176]{1,0:T(8,128)(2,1)S(1)} %whiten.1.own_ref), channel_id=1, source_target_pairs={{0,8},{2,10},{4,12},{6,14},{8,0},{10,2},{12,4},{14,6},{16,24},{18,... | collective-permute-start | bytes 417800 | tf_op jit(solution)/shard_map/ppermute | solution.py:206
  11.8 3.2 %collective-permute-start = (bf16[32,2176]{1,0:T(8,128)(2,1)S(1)}, bf16[32,2176]{1,0:T(8,128)(2,1)S(1)}, u32[]{:S(2)}, u32[]{:S(2)}) collective-permute-start(bf16[32,2176]{1,0:T(8,128)(2,1)S(1)} %whiten.1.own_ref), channel_id=1, source_target_pairs={{0,2},{2,0},{4,6},{6,4},{8,10},{10,8},{12,14},{14,12},{16,18},{18,... | collective-permute-start | bytes 417800 | tf_op jit(solution)/shard_map/ppermute | solution.py:206
  11.8 3.2 %collective-permute-start.8 = (bf16[32,2176]{1,0:T(8,128)(2,1)S(1)}, bf16[32,2176]{1,0:T(8,128)(2,1)S(1)}, u32[]{:S(2)}, u32[]{:S(2)}) collective-permute-start(bf16[32,2176]{1,0:T(8,128)(2,1)S(1)} %collective-permute-done.4.refs_3_), channel_id=1, source_target_pairs={{0,2},{2,0},{4,6},{6,4},{8,10},{10,8},{12,14},{14,12},{16,18},{18,... | collective-permute-start | bytes 417800 | tf_op jit(solution)/shard_map/ppermute | solution.py:206
  13.9 1.4 %collective-permute-start.7 = (bf16[32,2176]{1,0:T(8,128)(2,1)S(1)}, bf16[32,2176]{1,0:T(8,128)(2,1)S(1)}, u32[]{:S(2)}, u32[]{:S(2)}) collective-permute-start(bf16[32,2176]{1,0:T(8,128)(2,1)S(1)} %collective-permute-done.3.refs_2_), channel_id=1, source_target_pairs={{0,2},{2,0},{4,6},{6,4},{8,10},{10,8},{12,14},{14,12},{16,18},{18,... | collective-permute-start | bytes 417800 | tf_op jit(solution)/shard_map/ppermute | solution.py:206
  13.9 1.5 %collective-permute-start.6 = (bf16[32,2176]{1,0:T(8,128)(2,1)S(1)}, bf16[32,2176]{1,0:T(8,128)(2,1)S(1)}, u32[]{:S(2)}, u32[]{:S(2)}) collective-permute-start(bf16[32,2176]{1,0:T(8,128)(2,1)S(1)} %collective-permute-done.2.refs_1_), channel_id=1, source_target_pairs={{0,2},{2,0},{4,6},{6,4},{8,10},{10,8},{12,14},{14,12},{16,18},{18,... | collective-permute-start | bytes 417800 | tf_op jit(solution)/shard_map/ppermute | solution.py:206
  15.0 1.4 %collective-permute-start.5 = (bf16[32,2176]{1,0:T(8,128)(2,1)S(1)}, bf16[32,2176]{1,0:T(8,128)(2,1)S(1)}, u32[]{:S(2)}, u32[]{:S(2)}) collective-permute-start(bf16[32,2176]{1,0:T(8,128)(2,1)S(1)} %collective-permute-done.1.refs_0_), channel_id=1, source_target_pairs={{0,2},{2,0},{4,6},{6,4},{8,10},{10,8},{12,14},{14,12},{16,18},{18,... | collective-permute-start | bytes 417800 | tf_op jit(solution)/shard_map/ppermute | solution.py:206

commit v4 on v3

--- a/solution.py
+++ b/solution.py
@@ -226,12 +226,13 @@
     return i - 4 + 8 * (i // 4 % 2)
 
 
+SHARE = (2, 0, 1)
 TRADES = (partner_pair, other_pair, partner_far, other_far)
 
 
 def cross_kernel(order, own_ref, mate_ref, *refs):
-    arrived = [refs[at + order.index(k)] for at in (0, 4) for k in range(4)]
-    (ahead_hbm, behind_hbm, partners_ref, div_ahead, div_behind, count_ref, *products) = refs[8:-3]
+    arrived, shared = [refs[order.index(k)] for k in range(4)], [refs[4 + SHARE.index(k)] for k in range(3)]
+    (ahead_hbm, behind_hbm, partners_ref, div_ahead, div_behind, count_ref, *products) = refs[7:-3]
     ahead_ref, behind_ref, sems = refs[-3:]
     channels = own_ref.shape[0]
     packs = own_ref.shape[1] // LANES - 1
@@ -247,7 +248,8 @@
     def neighbours(lanes):
         pick = lambda a, b: jnp.where(first, a, b)
         own, mate = own_ref[:, lanes], mate_ref[:, lanes]
-        mine, theirs = [r[:, lanes] for r in arrived[:4]], [r[:, lanes] for r in arrived[4:]]
+        mine, theirs = [r[:, lanes] for r in arrived], [r[:, lanes] for r in shared]
+        theirs.append(theirs[2])
         met = [(pick(a, b), pick(b, a)) for a, b in zip(mine, theirs, strict=True)]
         met = [tuple(jnp.where(ok, x, jnp.zeros_like(x)) for x in blocks) for ok, blocks in zip(inside, met, strict=True)]
         choose = lambda up, a, b: tuple(jnp.where(up, x, y) for x, y in zip(a, b, strict=True))
@@ -387,9 +389,11 @@
     own = whiten(strain, channel_ok, window_ok, freq_devices)
     mate = trade(own, beside)
     arrived = [trade(own, partner) for partner in TRADES]
-    shared = [trade(block, beside) for block in arrived]
-    order = (2, 3, 0, 1)
-    last = [arrived[k] for k in order] + [shared[k] for k in order]
+    index = lax.axis_index("ch")
+    ahead_first = (index // 4 + index) % 2 == 0
+    shared = [trade(block, beside) for block in (*arrived[:2], jnp.where(ahead_first, arrived[2], arrived[3]))]
+    order = (3, 0, 2, 1)
+    last = [arrived[k] for k in order] + [shared[k] for k in SHARE]
     return cross([own, mate, *last], BINS // freq_devices, order)
 
 

time: 20.2 us -> 20.3 us (level)
  waiting for transfers between devices: 3.53 us -> 5.53 us
  starting transfers between devices: 8.73 us -> 6.73 us
    ppermute x9 -> x8, waiting for transfers between devices: 3.53 us -> 5.53 us  [trade(): lax.ppermute(value, 'ch', [(i, partner(i) if inside(i) else beside(i)) fo...]
    ppermute x9 -> x8, starting transfers between devices: 8.73 us -> 6.73 us  [trade(): lax.ppermute(value, 'ch', [(i, partner(i) if inside(i) else beside(i)) fo...]
  transfers between devices with their start and end apart: 9 -> 8, of which waited for: 5 -> 4; matrix products, arithmetic and copies ran while one was open for 0% -> 0% of each run, Pallas kernels for 0% -> 0%
where the time goes in v4:
time: 20.3 us; the launch traced here: 20.1 us
  Pallas kernels  7.16 us (35%)
  starting transfers between devices  6.73 us (33%)
  waiting for transfers between devices  5.53 us (27%)
  between operations  0.67 us (3%)
    ppermute x8, starting transfers between devices, trade(): lax.ppermute(value, 'ch', [(i, partner(i) if inside(i) else beside(i)) fo...  6.73 us
    ppermute x8, waiting for transfers between devices, trade(): lax.ppermute(value, 'ch', [(i, partner(i) if inside(i) else beside(i)) fo...  5.53 us
    pallas_call x1, Pallas kernels, cross(): pl.pallas_call(functools.partial(cross_kernel, order), in_specs=[pl.Block...  3.75 us
    pallas_call x1, Pallas kernels, whiten(): pl.pallas_call(whiten_kernel, in_specs=[pl.BlockSpec(memory_space=pltpu.H...  3.41 us
  transfers between devices with their start and end apart: 8, of which 4 were waited for; matrix products, arithmetic and copies ran while one was open for 0% of the time, Pallas kernels for 0%

profile of v4, /device:TPU:0, one launch (start us, length us, event | category | flops | bytes accessed | tf_op | source)
XLA Modules:
  0.0 20.1 jit_solution(2746145722722166198)
XLA Ops:
  0.6 3.4 %whiten.1.own_ref = bf16[32,2176]{1,0:T(8,128)(2,1)S(1)} custom-call(bf16[32,8,2048]{2,1,0:T(8,128)(2,1)} %x_hbm.1, s32[1,32]{1,0:T(1,128)} %bitcast.3, s32[8,32]{1,0:T(8,128)} %bitcast.2, bf16[2,2048,384]{2,1,0:T(8,128)(2,1)} %constant.37.clone.table_hbm, bf16[384,256]{1,0:T(8,128)(2,1)} %constant.38.clone.smooth_hbm), custom_call_target="tpu_custom_call" | custom-call | tf_op jit(solution)/shard_map/whiten/pallas_call | solution.py:175
  4.0 0.5 %collective-permute-start.4 = (bf16[32,2176]{1,0:T(8,128)(2,1)S(1)}, bf16[32,2176]{1,0:T(8,128)(2,1)S(1)}, u32[]{:S(2)}, u32[]{:S(2)}) collective-permute-start(bf16[32,2176]{1,0:T(8,128)(2,1)S(1)} %whiten.1.own_ref), channel_id=1, source_target_pairs={{0,2},{2,0},{4,8},{6,10},{8,4},{10,6},{12,16},{14,18},{16,12},{18,... | collective-permute-start | bytes 417800 | tf_op jit(solution)/shard_map/ppermute | solution.py:206
  4.6 4.0 %collective-permute-start.2 = (bf16[32,2176]{1,0:T(8,128)(2,1)S(1)}, bf16[32,2176]{1,0:T(8,128)(2,1)S(1)}, u32[]{:S(2)}, u32[]{:S(2)}) collective-permute-start(bf16[32,2176]{1,0:T(8,128)(2,1)S(1)} %whiten.1.own_ref), channel_id=1, source_target_pairs={{0,4},{2,6},{4,0},{6,2},{8,12},{10,14},{12,8},{14,10},{16,20},{18,... | collective-permute-start | bytes 417800 | tf_op jit(solution)/shard_map/ppermute | solution.py:206
  8.6 1.6 %collective-permute-start.3 = (bf16[32,2176]{1,0:T(8,128)(2,1)S(1)}, bf16[32,2176]{1,0:T(8,128)(2,1)S(1)}, u32[]{:S(2)}, u32[]{:S(2)}) collective-permute-start(bf16[32,2176]{1,0:T(8,128)(2,1)S(1)} %whiten.1.own_ref), channel_id=1, source_target_pairs={{0,8},{2,10},{4,12},{6,14},{8,0},{10,2},{12,4},{14,6},{16,24},{18,... | collective-permute-start | bytes 417800 | tf_op jit(solution)/shard_map/ppermute | solution.py:206
  10.2 0.0 collective-permute-start.1
  10.2 0.5 %collective-permute-start = (bf16[32,2176]{1,0:T(8,128)(2,1)S(1)}, bf16[32,2176]{1,0:T(8,128)(2,1)S(1)}, u32[]{:S(2)}, u32[]{:S(2)}) collective-permute-start(bf16[32,2176]{1,0:T(8,128)(2,1)S(1)} %whiten.1.own_ref), channel_id=1, source_target_pairs={{0,2},{2,0},{4,6},{6,4},{8,10},{10,8},{12,14},{14,12},{16,18},{18,... | collective-permute-start | bytes 417800 | tf_op jit(solution)/shard_map/ppermute | solution.py:206
  10.7 0.0 collective-permute-done.4.refs_3_
  10.7 0.0 collective-permute-start.7
  10.7 3.2 %collective-permute-done.2.refs_1_ = bf16[32,2176]{1,0:T(8,128)(2,1)S(1)} collective-permute-done((bf16[32,2176]{1,0:T(8,128)(2,1)S(1)}, bf16[32,2176]{1,0:T(8,128)(2,1)S(1)}, u32[]{:S(2)}, u32[]{:S(2)}) %collective-permute-start.2) | collective-permute-done | bytes 139296 | tf_op jit(solution)/shard_map/ppermute | solution.py:206
  13.9 0.0 collective-permute-start.6
  13.9 1.0 %collective-permute-done.3.refs_2_ = bf16[32,2176]{1,0:T(8,128)(2,1)S(1)} collective-permute-done((bf16[32,2176]{1,0:T(8,128)(2,1)S(1)}, bf16[32,2176]{1,0:T(8,128)(2,1)S(1)}, u32[]{:S(2)}, u32[]{:S(2)}) %collective-permute-start.3) | collective-permute-done | bytes 139296 | tf_op jit(solution)/shard_map/ppermute | solution.py:206
  14.9 0.0 collective-permute-done.1.refs_0_
  14.9 0.1 collective-permute-start.5
  15.0 0.0 collective-permute-done.mate_ref
  15.0 0.0 collective-permute-done.7.refs_6_
  15.0 0.2 %collective-permute-done.6.refs_5_ = bf16[32,2176]{1,0:T(8,128)(2,1)S(1)} collective-permute-done((bf16[32,2176]{1,0:T(8,128)(2,1)S(1)}, bf16[32,2176]{1,0:T(8,128)(2,1)S(1)}, u32[]{:S(2)}, u32[]{:S(2)}) %collective-permute-start.6) | collective-permute-done | bytes 139296 | tf_op jit(solution)/shard_map/ppermute | solution.py:206
  15.3 1.1 %collective-permute-done.5.refs_4_ = bf16[32,2176]{1,0:T(8,128)(2,1)S(1)} collective-permute-done((bf16[32,2176]{1,0:T(8,128)(2,1)S(1)}, bf16[32,2176]{1,0:T(8,128)(2,1)S(1)}, u32[]{:S(2)}, u32[]{:S(2)}) %collective-permute-start.5) | collective-permute-done | bytes 139296 | tf_op jit(solution)/shard_map/ppermute | solution.py:206
  16.4 3.7 %cross.1 = (bf16[2,128,32,128]{3,2,1,0:T(8,128)(2,1)}, bf16[2,128,32,128]{3,2,1,0:T(8,128)(2,1)}) custom-call(bf16[32,2176]{1,0:T(8,128)(2,1)S(1)} %whiten.1.own_ref, bf16[32,2176]{1,0:T(8,128)(2,1)S(1)} %collective-permute-done.mate_ref, bf16[32,2176]{1,0:T(8,128)(2,1)S(1)} %collective-permute-done.1.refs_0_, ...), custom_call_target="tpu_custom_call" | custom-call | tf_op jit(solution)/shard_map/cross/pallas_call | solution.py:365
  (1 shorter events, 0.0 us)
Async XLA Ops:
  4.0 6.6 %collective-permute-start.4 = (bf16[32,2176]{1,0:T(8,128)(2,1)S(1)}, bf16[32,2176]{1,0:T(8,128)(2,1)S(1)}, u32[]{:S(2)}, u32[]{:S(2)}) collective-permute-start(bf16[32,2176]{1,0:T(8,128)(2,1)S(1)} %whiten.1.own_ref), channel_id=1, source_target_pairs={{0,2},{2,0},{4,8},{6,10},{8,4},{10,6},{12,16},{14,18},{16,12},{18,... | collective-permute-start | bytes 417800 | tf_op jit(solution)/shard_map/ppermute | solution.py:206
  4.6 9.3 %collective-permute-start.2 = (bf16[32,2176]{1,0:T(8,128)(2,1)S(1)}, bf16[32,2176]{1,0:T(8,128)(2,1)S(1)}, u32[]{:S(2)}, u32[]{:S(2)}) collective-permute-start(bf16[32,2176]{1,0:T(8,128)(2,1)S(1)} %whiten.1.own_ref), channel_id=1, source_target_pairs={{0,4},{2,6},{4,0},{6,2},{8,12},{10,14},{12,8},{14,10},{16,20},{18,... | collective-permute-start | bytes 417800 | tf_op jit(solution)/shard_map/ppermute | solution.py:206
  8.6 6.3 %collective-permute-start.3 = (bf16[32,2176]{1,0:T(8,128)(2,1)S(1)}, bf16[32,2176]{1,0:T(8,128)(2,1)S(1)}, u32[]{:S(2)}, u32[]{:S(2)}) collective-permute-start(bf16[32,2176]{1,0:T(8,128)(2,1)S(1)} %whiten.1.own_ref), channel_id=1, source_target_pairs={{0,8},{2,10},{4,12},{6,14},{8,0},{10,2},{12,4},{14,6},{16,24},{18,... | collective-permute-start | bytes 417800 | tf_op jit(solution)/shard_map/ppermute | solution.py:206
  10.2 4.7 %collective-permute-start.1 = (bf16[32,2176]{1,0:T(8,128)(2,1)S(1)}, bf16[32,2176]{1,0:T(8,128)(2,1)S(1)}, u32[]{:S(2)}, u32[]{:S(2)}) collective-permute-start(bf16[32,2176]{1,0:T(8,128)(2,1)S(1)} %whiten.1.own_ref), channel_id=1, source_target_pairs={{0,2},{2,0},{4,6},{6,4},{8,16},{10,18},{12,20},{14,22},{16,8},{18,... | collective-permute-start | bytes 417800 | tf_op jit(solution)/shard_map/ppermute | solution.py:206
  10.2 4.8 %collective-permute-start = (bf16[32,2176]{1,0:T(8,128)(2,1)S(1)}, bf16[32,2176]{1,0:T(8,128)(2,1)S(1)}, u32[]{:S(2)}, u32[]{:S(2)}) collective-permute-start(bf16[32,2176]{1,0:T(8,128)(2,1)S(1)} %whiten.1.own_ref), channel_id=1, source_target_pairs={{0,2},{2,0},{4,6},{6,4},{8,10},{10,8},{12,14},{14,12},{16,18},{18,... | collective-permute-start | bytes 417800 | tf_op jit(solution)/shard_map/ppermute | solution.py:206
  10.7 4.3 %collective-permute-start.7 = (bf16[32,2176]{1,0:T(8,128)(2,1)S(1)}, bf16[32,2176]{1,0:T(8,128)(2,1)S(1)}, u32[]{:S(2)}, u32[]{:S(2)}) collective-permute-start(bf16[32,2176]{1,0:T(8,128)(2,1)S(1)} %collective-permute-done.4.refs_3_), channel_id=1, source_target_pairs={{0,2},{2,0},{4,6},{6,4},{8,10},{10,8},{12,14},{14,12},{16,18},{18,... | collective-permute-start | bytes 417800 | tf_op jit(solution)/shard_map/ppermute | solution.py:206
  13.9 1.4 %collective-permute-start.6 = (bf16[32,2176]{1,0:T(8,128)(2,1)S(1)}, bf16[32,2176]{1,0:T(8,128)(2,1)S(1)}, u32[]{:S(2)}, u32[]{:S(2)}) collective-permute-start(bf16[32,2176]{1,0:T(8,128)(2,1)S(1)} %collective-permute-done.2.refs_1_), channel_id=1, source_target_pairs={{0,2},{2,0},{4,6},{6,4},{8,10},{10,8},{12,14},{14,12},{16,18},{18,... | collective-permute-start | bytes 417800 | tf_op jit(solution)/shard_map/ppermute | solution.py:206
  14.9 1.4 %collective-permute-start.5 = (bf16[32,2176]{1,0:T(8,128)(2,1)S(1)}, bf16[32,2176]{1,0:T(8,128)(2,1)S(1)}, u32[]{:S(2)}, u32[]{:S(2)}) collective-permute-start(bf16[32,2176]{1,0:T(8,128)(2,1)S(1)} %broadcast_select_fusion), channel_id=1, source_target_pairs={{0,2},{2,0},{4,6},{6,4},{8,10},{10,8},{12,14},{14,12},{16,18},{18,... | collective-permute-start | bytes 417800 | tf_op jit(solution)/shard_map/ppermute | solution.py:206

commit v5 on v4

--- a/solution.py
+++ b/solution.py
@@ -139,11 +139,7 @@
         part = slice(h * half * windows, (h + 1) * half * windows)
         spectra = jnp.dot(level_ref[part], table_ref[...], preferred_element_type=jnp.float32)
         power = spectra * spectra
-        high = power.astype(jnp.bfloat16)
-        low = (power - high.astype(jnp.float32)).astype(jnp.bfloat16)
-        smooth = jnp.dot(high, ones, preferred_element_type=jnp.float32) + jnp.dot(
-            low, ones, preferred_element_type=jnp.float32
-        )
+        smooth = jnp.dot(power.astype(jnp.bfloat16), ones, preferred_element_type=jnp.float32)
         white = spectra[:, halo:] * lax.rsqrt(smooth * (1.0 / (2 * BIN_HALF + 1)) + 1e-06)
         for t in range(0, own, LANES):
             tile_width = min(LANES, own - t)
@@ -314,11 +310,14 @@
             lhs, partners_ref[:, lanes], contract, preferred_element_type=jnp.float32
         )
 
-    def copies(g):
-        bins = pl.ds(g * PACK, PACK)
+    ends = sorted({1, packs - 1, packs, *range(2, packs, 2)})
+
+    def copies(k):
+        start = ends[k - 1] if k else 0
+        bins = pl.ds(start * PACK, (ends[k] - start) * PACK)
         return [
-            pltpu.make_async_copy(held.at[:, bins], out.at[:, bins], sems.at[k, g])
-            for k, (held, out) in enumerate(((ahead_ref, ahead_hbm), (behind_ref, behind_hbm)))
+            pltpu.make_async_copy(held.at[:, bins], out.at[:, bins], sems.at[q, k])
+            for q, (held, out) in enumerate(((ahead_ref, ahead_hbm), (behind_ref, behind_hbm)))
         ]
 
     def finish(g):
@@ -329,8 +328,9 @@
                 ahead, behind = skewed(*(product[rows, pl.ds(t * LANES, LANES)] for t in range(3)))
                 ahead_ref[v, g * PACK + f] = (ahead * div_ahead[...]).astype(jnp.bfloat16)
                 behind_ref[v, g * PACK + f] = (behind * div_behind[...]).astype(jnp.bfloat16)
-        for copy in copies(g):
-            copy.start()
+        if g + 1 in ends:
+            for copy in copies(ends.index(g + 1)):
+                copy.start()
 
     flags = slice(packs * LANES, (packs + 1) * LANES)
     lead_packs = WIDE // LANES
@@ -352,8 +352,8 @@
         if g + 2 < packs:
             multiply(g + 2)
         finish(g)
-    for g in range(packs):
-        for copy in copies(g):
+    for k in range(len(ends)):
+        for copy in copies(k):
             copy.wait()
 
 

time: 20.3 us -> 20.1 us (level)
  no operation moved by 1% of the time
where the time goes in v5:
time: 20.1 us; the launch traced here: 19.9 us
  Pallas kernels  6.99 us (35%)
  starting transfers between devices  6.72 us (33%)
  waiting for transfers between devices  5.53 us (28%)
  between operations  0.67 us (3%)
    ppermute x8, starting transfers between devices, trade(): lax.ppermute(value, 'ch', [(i, partner(i) if inside(i) else beside(i)) fo...  6.72 us
    ppermute x8, waiting for transfers between devices, trade(): lax.ppermute(value, 'ch', [(i, partner(i) if inside(i) else beside(i)) fo...  5.53 us
    pallas_call x1, Pallas kernels, cross(): pl.pallas_call(functools.partial(cross_kernel, order), in_specs=[pl.Block...  3.75 us
    pallas_call x1, Pallas kernels, whiten(): pl.pallas_call(whiten_kernel, in_specs=[pl.BlockSpec(memory_space=pltpu.H...  3.24 us
  transfers between devices with their start and end apart: 8, of which 4 were waited for; matrix products, arithmetic and copies ran while one was open for 0% of the time, Pallas kernels for 0%

profile of v5, /device:TPU:0, one launch (start us, length us, event | category | flops | bytes accessed | tf_op | source)
XLA Modules:
  0.0 19.9 jit_solution(8961884756340379834)
XLA Ops:
  0.6 3.2 %whiten.1.own_ref = bf16[32,2176]{1,0:T(8,128)(2,1)S(1)} custom-call(bf16[32,8,2048]{2,1,0:T(8,128)(2,1)} %x_hbm.1, s32[1,32]{1,0:T(1,128)} %bitcast.3, s32[8,32]{1,0:T(8,128)} %bitcast.2, bf16[2,2048,384]{2,1,0:T(8,128)(2,1)} %constant.37.clone.table_hbm, bf16[384,256]{1,0:T(8,128)(2,1)} %constant.38.clone.smooth_hbm), custom_call_target="tpu_custom_call" | custom-call | tf_op jit(solution)/shard_map/whiten/pallas_call | solution.py:171
  3.9 0.5 %collective-permute-start.4 = (bf16[32,2176]{1,0:T(8,128)(2,1)S(1)}, bf16[32,2176]{1,0:T(8,128)(2,1)S(1)}, u32[]{:S(2)}, u32[]{:S(2)}) collective-permute-start(bf16[32,2176]{1,0:T(8,128)(2,1)S(1)} %whiten.1.own_ref), channel_id=1, source_target_pairs={{0,2},{2,0},{4,8},{6,10},{8,4},{10,6},{12,16},{14,18},{16,12},{18,... | collective-permute-start | bytes 417800 | tf_op jit(solution)/shard_map/ppermute | solution.py:202
  4.4 4.0 %collective-permute-start.2 = (bf16[32,2176]{1,0:T(8,128)(2,1)S(1)}, bf16[32,2176]{1,0:T(8,128)(2,1)S(1)}, u32[]{:S(2)}, u32[]{:S(2)}) collective-permute-start(bf16[32,2176]{1,0:T(8,128)(2,1)S(1)} %whiten.1.own_ref), channel_id=1, source_target_pairs={{0,4},{2,6},{4,0},{6,2},{8,12},{10,14},{12,8},{14,10},{16,20},{18,... | collective-permute-start | bytes 417800 | tf_op jit(solution)/shard_map/ppermute | solution.py:202
  8.4 1.6 %collective-permute-start.3 = (bf16[32,2176]{1,0:T(8,128)(2,1)S(1)}, bf16[32,2176]{1,0:T(8,128)(2,1)S(1)}, u32[]{:S(2)}, u32[]{:S(2)}) collective-permute-start(bf16[32,2176]{1,0:T(8,128)(2,1)S(1)} %whiten.1.own_ref), channel_id=1, source_target_pairs={{0,8},{2,10},{4,12},{6,14},{8,0},{10,2},{12,4},{14,6},{16,24},{18,... | collective-permute-start | bytes 417800 | tf_op jit(solution)/shard_map/ppermute | solution.py:202
  10.0 0.0 collective-permute-start.1
  10.0 0.5 %collective-permute-start = (bf16[32,2176]{1,0:T(8,128)(2,1)S(1)}, bf16[32,2176]{1,0:T(8,128)(2,1)S(1)}, u32[]{:S(2)}, u32[]{:S(2)}) collective-permute-start(bf16[32,2176]{1,0:T(8,128)(2,1)S(1)} %whiten.1.own_ref), channel_id=1, source_target_pairs={{0,2},{2,0},{4,6},{6,4},{8,10},{10,8},{12,14},{14,12},{16,18},{18,... | collective-permute-start | bytes 417800 | tf_op jit(solution)/shard_map/ppermute | solution.py:202
  10.5 0.0 collective-permute-done.4.refs_3_
  10.5 0.0 collective-permute-start.7
  10.5 3.2 %collective-permute-done.2.refs_1_ = bf16[32,2176]{1,0:T(8,128)(2,1)S(1)} collective-permute-done((bf16[32,2176]{1,0:T(8,128)(2,1)S(1)}, bf16[32,2176]{1,0:T(8,128)(2,1)S(1)}, u32[]{:S(2)}, u32[]{:S(2)}) %collective-permute-start.2) | collective-permute-done | bytes 139296 | tf_op jit(solution)/shard_map/ppermute | solution.py:202
  13.7 0.0 collective-permute-start.6
  13.7 1.0 %collective-permute-done.3.refs_2_ = bf16[32,2176]{1,0:T(8,128)(2,1)S(1)} collective-permute-done((bf16[32,2176]{1,0:T(8,128)(2,1)S(1)}, bf16[32,2176]{1,0:T(8,128)(2,1)S(1)}, u32[]{:S(2)}, u32[]{:S(2)}) %collective-permute-start.3) | collective-permute-done | bytes 139296 | tf_op jit(solution)/shard_map/ppermute | solution.py:202
  14.7 0.0 collective-permute-done.1.refs_0_
  14.8 0.1 collective-permute-start.5
  14.8 0.0 collective-permute-done.mate_ref
  14.9 0.0 collective-permute-done.7.refs_6_
  14.9 0.2 %collective-permute-done.6.refs_5_ = bf16[32,2176]{1,0:T(8,128)(2,1)S(1)} collective-permute-done((bf16[32,2176]{1,0:T(8,128)(2,1)S(1)}, bf16[32,2176]{1,0:T(8,128)(2,1)S(1)}, u32[]{:S(2)}, u32[]{:S(2)}) %collective-permute-start.6) | collective-permute-done | bytes 139296 | tf_op jit(solution)/shard_map/ppermute | solution.py:202
  15.1 1.1 %collective-permute-done.5.refs_4_ = bf16[32,2176]{1,0:T(8,128)(2,1)S(1)} collective-permute-done((bf16[32,2176]{1,0:T(8,128)(2,1)S(1)}, bf16[32,2176]{1,0:T(8,128)(2,1)S(1)}, u32[]{:S(2)}, u32[]{:S(2)}) %collective-permute-start.5) | collective-permute-done | bytes 139296 | tf_op jit(solution)/shard_map/ppermute | solution.py:202
  16.2 3.8 %cross.1 = (bf16[2,128,32,128]{3,2,1,0:T(8,128)(2,1)}, bf16[2,128,32,128]{3,2,1,0:T(8,128)(2,1)}) custom-call(bf16[32,2176]{1,0:T(8,128)(2,1)S(1)} %whiten.1.own_ref, bf16[32,2176]{1,0:T(8,128)(2,1)S(1)} %collective-permute-done.mate_ref, bf16[32,2176]{1,0:T(8,128)(2,1)S(1)} %collective-permute-done.1.refs_0_, ...), custom_call_target="tpu_custom_call" | custom-call | tf_op jit(solution)/shard_map/cross/pallas_call | solution.py:365
  (1 shorter events, 0.0 us)
Async XLA Ops:
  3.9 6.6 %collective-permute-start.4 = (bf16[32,2176]{1,0:T(8,128)(2,1)S(1)}, bf16[32,2176]{1,0:T(8,128)(2,1)S(1)}, u32[]{:S(2)}, u32[]{:S(2)}) collective-permute-start(bf16[32,2176]{1,0:T(8,128)(2,1)S(1)} %whiten.1.own_ref), channel_id=1, source_target_pairs={{0,2},{2,0},{4,8},{6,10},{8,4},{10,6},{12,16},{14,18},{16,12},{18,... | collective-permute-start | bytes 417800 | tf_op jit(solution)/shard_map/ppermute | solution.py:202
  4.4 9.3 %collective-permute-start.2 = (bf16[32,2176]{1,0:T(8,128)(2,1)S(1)}, bf16[32,2176]{1,0:T(8,128)(2,1)S(1)}, u32[]{:S(2)}, u32[]{:S(2)}) collective-permute-start(bf16[32,2176]{1,0:T(8,128)(2,1)S(1)} %whiten.1.own_ref), channel_id=1, source_target_pairs={{0,4},{2,6},{4,0},{6,2},{8,12},{10,14},{12,8},{14,10},{16,20},{18,... | collective-permute-start | bytes 417800 | tf_op jit(solution)/shard_map/ppermute | solution.py:202
  8.4 6.3 %collective-permute-start.3 = (bf16[32,2176]{1,0:T(8,128)(2,1)S(1)}, bf16[32,2176]{1,0:T(8,128)(2,1)S(1)}, u32[]{:S(2)}, u32[]{:S(2)}) collective-permute-start(bf16[32,2176]{1,0:T(8,128)(2,1)S(1)} %whiten.1.own_ref), channel_id=1, source_target_pairs={{0,8},{2,10},{4,12},{6,14},{8,0},{10,2},{12,4},{14,6},{16,24},{18,... | collective-permute-start | bytes 417800 | tf_op jit(solution)/shard_map/ppermute | solution.py:202
  10.0 4.7 %collective-permute-start.1 = (bf16[32,2176]{1,0:T(8,128)(2,1)S(1)}, bf16[32,2176]{1,0:T(8,128)(2,1)S(1)}, u32[]{:S(2)}, u32[]{:S(2)}) collective-permute-start(bf16[32,2176]{1,0:T(8,128)(2,1)S(1)} %whiten.1.own_ref), channel_id=1, source_target_pairs={{0,2},{2,0},{4,6},{6,4},{8,16},{10,18},{12,20},{14,22},{16,8},{18,... | collective-permute-start | bytes 417800 | tf_op jit(solution)/shard_map/ppermute | solution.py:202
  10.0 4.8 %collective-permute-start = (bf16[32,2176]{1,0:T(8,128)(2,1)S(1)}, bf16[32,2176]{1,0:T(8,128)(2,1)S(1)}, u32[]{:S(2)}, u32[]{:S(2)}) collective-permute-start(bf16[32,2176]{1,0:T(8,128)(2,1)S(1)} %whiten.1.own_ref), channel_id=1, source_target_pairs={{0,2},{2,0},{4,6},{6,4},{8,10},{10,8},{12,14},{14,12},{16,18},{18,... | collective-permute-start | bytes 417800 | tf_op jit(solution)/shard_map/ppermute | solution.py:202
  10.5 4.3 %collective-permute-start.7 = (bf16[32,2176]{1,0:T(8,128)(2,1)S(1)}, bf16[32,2176]{1,0:T(8,128)(2,1)S(1)}, u32[]{:S(2)}, u32[]{:S(2)}) collective-permute-start(bf16[32,2176]{1,0:T(8,128)(2,1)S(1)} %collective-permute-done.4.refs_3_), channel_id=1, source_target_pairs={{0,2},{2,0},{4,6},{6,4},{8,10},{10,8},{12,14},{14,12},{16,18},{18,... | collective-permute-start | bytes 417800 | tf_op jit(solution)/shard_map/ppermute | solution.py:202
  13.7 1.4 %collective-permute-start.6 = (bf16[32,2176]{1,0:T(8,128)(2,1)S(1)}, bf16[32,2176]{1,0:T(8,128)(2,1)S(1)}, u32[]{:S(2)}, u32[]{:S(2)}) collective-permute-start(bf16[32,2176]{1,0:T(8,128)(2,1)S(1)} %collective-permute-done.2.refs_1_), channel_id=1, source_target_pairs={{0,2},{2,0},{4,6},{6,4},{8,10},{10,8},{12,14},{14,12},{16,18},{18,... | collective-permute-start | bytes 417800 | tf_op jit(solution)/shard_map/ppermute | solution.py:202
  14.8 1.4 %collective-permute-start.5 = (bf16[32,2176]{1,0:T(8,128)(2,1)S(1)}, bf16[32,2176]{1,0:T(8,128)(2,1)S(1)}, u32[]{:S(2)}, u32[]{:S(2)}) collective-permute-start(bf16[32,2176]{1,0:T(8,128)(2,1)S(1)} %broadcast_select_fusion), channel_id=1, source_target_pairs={{0,2},{2,0},{4,6},{6,4},{8,10},{10,8},{12,14},{14,12},{16,18},{18,... | collective-permute-start | bytes 417800 | tf_op jit(solution)/shard_map/ppermute | solution.py:202

commit v6 on v5

--- a/solution.py
+++ b/solution.py
@@ -51,14 +51,8 @@
     return np.stack(tables)
 
 
-def smoother(bin_count):
-    bins, _ = bin_columns(bin_count)
-    own = bins[4 * BIN_HALF :]
-    return (np.abs(bins[:, None] - own[None, :]) <= BIN_HALF).astype(ml_dtypes.bfloat16)
-
-
 def whiten_kernel(
-    x_hbm, ok_hbm, win_hbm, table_hbm, smooth_hbm, out_ref,
+    x_hbm, ok_hbm, win_hbm, table_hbm, out_ref,
     x_ref, ok_ref, win_ref, table_ref, smooth_ref, mag_ref, level_ref, spec_ref, x_sems, table_sems, sems,
 ):
     channels, windows, samples = x_ref.shape
@@ -84,7 +78,7 @@
     small_copies = [
         pltpu.make_async_copy(source, target, sems.at[k])
         for k, (source, target) in enumerate(
-            ((ok_hbm, ok_ref), (win_hbm, win_ref), (smooth_hbm, smooth_ref))
+            ((ok_hbm, ok_ref), (win_hbm, win_ref))
         )
     ]
     for copy in x_copies + table_copies + small_copies:
@@ -95,6 +89,18 @@
     source = lax.broadcasted_iota(jnp.int32, (2 * tile, tile), 0) - TIME_HALF
     target = lax.broadcasted_iota(jnp.int32, (2 * tile, tile), 1)
     band = (jnp.abs(source - target) <= TIME_HALF).astype(jnp.float32).astype(jnp.bfloat16)
+
+    def bin_of(column):
+        packed = column - halo
+        beyond = lax.rem(column, 2 * BIN_HALF) - BIN_HALF
+        beyond = jnp.where(beyond < 0, beyond, beyond + own // 2)
+        return jnp.where(packed < 0, beyond, packed // (2 * PACK) * PACK + lax.rem(packed, PACK))
+
+    shape = (own + halo, own)
+    apart = bin_of(lax.broadcasted_iota(jnp.int32, shape, 0)) - bin_of(
+        lax.broadcasted_iota(jnp.int32, shape, 1) + halo
+    )
+    smooth_ref[...] = (jnp.abs(apart) <= BIN_HALF).astype(jnp.float32).astype(jnp.bfloat16)
 
     def loaded(t):
         return x_ref[:, :, t * tile : (t + 1) * tile].astype(jnp.float32).reshape(rows, tile)
@@ -163,14 +169,13 @@
     channels, windows, samples = strain.shape
     bin_count = BINS // freq_devices
     tables = jnp.asarray(dft_tables(freq_devices, samples))
-    ones = jnp.asarray(smoother(bin_count))
     columns = tables.shape[2]
     own = 2 * bin_count
     rows = channels * windows
     chunks = samples // CHUNK
     return pl.pallas_call(
         whiten_kernel,
-        in_specs=[pl.BlockSpec(memory_space=pltpu.HBM)] * 5,
+        in_specs=[pl.BlockSpec(memory_space=pltpu.HBM)] * 4,
         out_specs=pl.BlockSpec(memory_space=pltpu.VMEM),
         out_shape=pltpu.VMEM((channels, windows * own + LANES), jnp.bfloat16),
         scratch_shapes=[
@@ -184,14 +189,14 @@
             pltpu.VMEM((HALVES, -(-own // LANES), rows // HALVES, LANES), jnp.float32),
             pltpu.SemaphoreType.DMA((chunks,)),
             pltpu.SemaphoreType.DMA((chunks,)),
-            pltpu.SemaphoreType.DMA((3,)),
+            pltpu.SemaphoreType.DMA((2,)),
         ],
         compiler_params=pltpu.CompilerParams(vmem_limit_bytes=VMEM_BYTES),
         name="whiten",
     )(
         *(
             pltpu.with_memory_space_constraint(value, pltpu.HBM)
-            for value in (strain, channel_ok.reshape(1, channels), window_ok.T, tables, ones)
+            for value in (strain, channel_ok.reshape(1, channels), window_ok.T, tables)
         )
     )
 

time: 20.1 us -> 20.1 us (level)
  no operation moved by 1% of the time
where the time goes in v6:
time: 20.1 us; the launch traced here: 19.9 us
  Pallas kernels  6.96 us (35%)
  starting transfers between devices  6.73 us (33%)
  waiting for transfers between devices  5.53 us (28%)
  between operations  0.67 us (3%)
    ppermute x8, starting transfers between devices, trade(): lax.ppermute(value, 'ch', [(i, partner(i) if inside(i) else beside(i)) fo...  6.73 us
    ppermute x8, waiting for transfers between devices, trade(): lax.ppermute(value, 'ch', [(i, partner(i) if inside(i) else beside(i)) fo...  5.53 us
    pallas_call x1, Pallas kernels, cross(): pl.pallas_call(functools.partial(cross_kernel, order), in_specs=[pl.Block...  3.75 us
    pallas_call x1, Pallas kernels, whiten(): pl.pallas_call(whiten_kernel, in_specs=[pl.BlockSpec(memory_space=pltpu.H...  3.2 us
  transfers between devices with their start and end apart: 8, of which 4 were waited for; matrix products, arithmetic and copies ran while one was open for 0% of the time, Pallas kernels for 0%

profile of v6, /device:TPU:0, one launch (start us, length us, event | category | flops | bytes accessed | tf_op | source)
XLA Modules:
  0.0 19.9 jit_solution(16585036068780687846)
XLA Ops:
  0.6 3.2 %whiten.1.own_ref = bf16[32,2176]{1,0:T(8,128)(2,1)S(1)} custom-call(bf16[32,8,2048]{2,1,0:T(8,128)(2,1)} %x_hbm.1, s32[1,32]{1,0:T(1,128)} %bitcast.3, s32[8,32]{1,0:T(8,128)} %bitcast.2, bf16[2,2048,384]{2,1,0:T(8,128)(2,1)} %constant.35.clone.table_hbm), custom_call_target="tpu_custom_call" | custom-call | tf_op jit(solution)/shard_map/whiten/pallas_call | solution.py:176
  3.8 0.5 %collective-permute-start.4 = (bf16[32,2176]{1,0:T(8,128)(2,1)S(1)}, bf16[32,2176]{1,0:T(8,128)(2,1)S(1)}, u32[]{:S(2)}, u32[]{:S(2)}) collective-permute-start(bf16[32,2176]{1,0:T(8,128)(2,1)S(1)} %whiten.1.own_ref), channel_id=1, source_target_pairs={{0,2},{2,0},{4,8},{6,10},{8,4},{10,6},{12,16},{14,18},{16,12},{18,... | collective-permute-start | bytes 417800 | tf_op jit(solution)/shard_map/ppermute | solution.py:207
  4.4 4.0 %collective-permute-start.2 = (bf16[32,2176]{1,0:T(8,128)(2,1)S(1)}, bf16[32,2176]{1,0:T(8,128)(2,1)S(1)}, u32[]{:S(2)}, u32[]{:S(2)}) collective-permute-start(bf16[32,2176]{1,0:T(8,128)(2,1)S(1)} %whiten.1.own_ref), channel_id=1, source_target_pairs={{0,4},{2,6},{4,0},{6,2},{8,12},{10,14},{12,8},{14,10},{16,20},{18,... | collective-permute-start | bytes 417800 | tf_op jit(solution)/shard_map/ppermute | solution.py:207
  8.4 1.6 %collective-permute-start.3 = (bf16[32,2176]{1,0:T(8,128)(2,1)S(1)}, bf16[32,2176]{1,0:T(8,128)(2,1)S(1)}, u32[]{:S(2)}, u32[]{:S(2)}) collective-permute-start(bf16[32,2176]{1,0:T(8,128)(2,1)S(1)} %whiten.1.own_ref), channel_id=1, source_target_pairs={{0,8},{2,10},{4,12},{6,14},{8,0},{10,2},{12,4},{14,6},{16,24},{18,... | collective-permute-start | bytes 417800 | tf_op jit(solution)/shard_map/ppermute | solution.py:207
  10.0 0.0 collective-permute-start.1
  10.0 0.5 %collective-permute-start = (bf16[32,2176]{1,0:T(8,128)(2,1)S(1)}, bf16[32,2176]{1,0:T(8,128)(2,1)S(1)}, u32[]{:S(2)}, u32[]{:S(2)}) collective-permute-start(bf16[32,2176]{1,0:T(8,128)(2,1)S(1)} %whiten.1.own_ref), channel_id=1, source_target_pairs={{0,2},{2,0},{4,6},{6,4},{8,10},{10,8},{12,14},{14,12},{16,18},{18,... | collective-permute-start | bytes 417800 | tf_op jit(solution)/shard_map/ppermute | solution.py:207
  10.5 0.0 collective-permute-done.4.refs_3_
  10.5 0.0 collective-permute-start.7
  10.5 3.2 %collective-permute-done.2.refs_1_ = bf16[32,2176]{1,0:T(8,128)(2,1)S(1)} collective-permute-done((bf16[32,2176]{1,0:T(8,128)(2,1)S(1)}, bf16[32,2176]{1,0:T(8,128)(2,1)S(1)}, u32[]{:S(2)}, u32[]{:S(2)}) %collective-permute-start.2) | collective-permute-done | bytes 139296 | tf_op jit(solution)/shard_map/ppermute | solution.py:207
  13.7 0.0 collective-permute-start.6
  13.7 1.0 %collective-permute-done.3.refs_2_ = bf16[32,2176]{1,0:T(8,128)(2,1)S(1)} collective-permute-done((bf16[32,2176]{1,0:T(8,128)(2,1)S(1)}, bf16[32,2176]{1,0:T(8,128)(2,1)S(1)}, u32[]{:S(2)}, u32[]{:S(2)}) %collective-permute-start.3) | collective-permute-done | bytes 139296 | tf_op jit(solution)/shard_map/ppermute | solution.py:207
  14.7 0.0 collective-permute-done.1.refs_0_
  14.7 0.1 collective-permute-start.5
  14.8 0.0 collective-permute-done.mate_ref
  14.8 0.0 collective-permute-done.7.refs_6_
  14.8 0.2 %collective-permute-done.6.refs_5_ = bf16[32,2176]{1,0:T(8,128)(2,1)S(1)} collective-permute-done((bf16[32,2176]{1,0:T(8,128)(2,1)S(1)}, bf16[32,2176]{1,0:T(8,128)(2,1)S(1)}, u32[]{:S(2)}, u32[]{:S(2)}) %collective-permute-start.6) | collective-permute-done | bytes 139296 | tf_op jit(solution)/shard_map/ppermute | solution.py:207
  15.0 1.1 %collective-permute-done.5.refs_4_ = bf16[32,2176]{1,0:T(8,128)(2,1)S(1)} collective-permute-done((bf16[32,2176]{1,0:T(8,128)(2,1)S(1)}, bf16[32,2176]{1,0:T(8,128)(2,1)S(1)}, u32[]{:S(2)}, u32[]{:S(2)}) %collective-permute-start.5) | collective-permute-done | bytes 139296 | tf_op jit(solution)/shard_map/ppermute | solution.py:207
  16.2 3.8 %cross.1 = (bf16[2,128,32,128]{3,2,1,0:T(8,128)(2,1)}, bf16[2,128,32,128]{3,2,1,0:T(8,128)(2,1)}) custom-call(bf16[32,2176]{1,0:T(8,128)(2,1)S(1)} %whiten.1.own_ref, bf16[32,2176]{1,0:T(8,128)(2,1)S(1)} %collective-permute-done.mate_ref, bf16[32,2176]{1,0:T(8,128)(2,1)S(1)} %collective-permute-done.1.refs_0_, ...), custom_call_target="tpu_custom_call" | custom-call | tf_op jit(solution)/shard_map/cross/pallas_call | solution.py:370
  (1 shorter events, 0.0 us)
Async XLA Ops:
  3.8 6.6 %collective-permute-start.4 = (bf16[32,2176]{1,0:T(8,128)(2,1)S(1)}, bf16[32,2176]{1,0:T(8,128)(2,1)S(1)}, u32[]{:S(2)}, u32[]{:S(2)}) collective-permute-start(bf16[32,2176]{1,0:T(8,128)(2,1)S(1)} %whiten.1.own_ref), channel_id=1, source_target_pairs={{0,2},{2,0},{4,8},{6,10},{8,4},{10,6},{12,16},{14,18},{16,12},{18,... | collective-permute-start | bytes 417800 | tf_op jit(solution)/shard_map/ppermute | solution.py:207
  4.4 9.3 %collective-permute-start.2 = (bf16[32,2176]{1,0:T(8,128)(2,1)S(1)}, bf16[32,2176]{1,0:T(8,128)(2,1)S(1)}, u32[]{:S(2)}, u32[]{:S(2)}) collective-permute-start(bf16[32,2176]{1,0:T(8,128)(2,1)S(1)} %whiten.1.own_ref), channel_id=1, source_target_pairs={{0,4},{2,6},{4,0},{6,2},{8,12},{10,14},{12,8},{14,10},{16,20},{18,... | collective-permute-start | bytes 417800 | tf_op jit(solution)/shard_map/ppermute | solution.py:207
  8.4 6.3 %collective-permute-start.3 = (bf16[32,2176]{1,0:T(8,128)(2,1)S(1)}, bf16[32,2176]{1,0:T(8,128)(2,1)S(1)}, u32[]{:S(2)}, u32[]{:S(2)}) collective-permute-start(bf16[32,2176]{1,0:T(8,128)(2,1)S(1)} %whiten.1.own_ref), channel_id=1, source_target_pairs={{0,8},{2,10},{4,12},{6,14},{8,0},{10,2},{12,4},{14,6},{16,24},{18,... | collective-permute-start | bytes 417800 | tf_op jit(solution)/shard_map/ppermute | solution.py:207
  10.0 4.7 %collective-permute-start.1 = (bf16[32,2176]{1,0:T(8,128)(2,1)S(1)}, bf16[32,2176]{1,0:T(8,128)(2,1)S(1)}, u32[]{:S(2)}, u32[]{:S(2)}) collective-permute-start(bf16[32,2176]{1,0:T(8,128)(2,1)S(1)} %whiten.1.own_ref), channel_id=1, source_target_pairs={{0,2},{2,0},{4,6},{6,4},{8,16},{10,18},{12,20},{14,22},{16,8},{18,... | collective-permute-start | bytes 417800 | tf_op jit(solution)/shard_map/ppermute | solution.py:207
  10.0 4.8 %collective-permute-start = (bf16[32,2176]{1,0:T(8,128)(2,1)S(1)}, bf16[32,2176]{1,0:T(8,128)(2,1)S(1)}, u32[]{:S(2)}, u32[]{:S(2)}) collective-permute-start(bf16[32,2176]{1,0:T(8,128)(2,1)S(1)} %whiten.1.own_ref), channel_id=1, source_target_pairs={{0,2},{2,0},{4,6},{6,4},{8,10},{10,8},{12,14},{14,12},{16,18},{18,... | collective-permute-start | bytes 417800 | tf_op jit(solution)/shard_map/ppermute | solution.py:207
  10.5 4.3 %collective-permute-start.7 = (bf16[32,2176]{1,0:T(8,128)(2,1)S(1)}, bf16[32,2176]{1,0:T(8,128)(2,1)S(1)}, u32[]{:S(2)}, u32[]{:S(2)}) collective-permute-start(bf16[32,2176]{1,0:T(8,128)(2,1)S(1)} %collective-permute-done.4.refs_3_), channel_id=1, source_target_pairs={{0,2},{2,0},{4,6},{6,4},{8,10},{10,8},{12,14},{14,12},{16,18},{18,... | collective-permute-start | bytes 417800 | tf_op jit(solution)/shard_map/ppermute | solution.py:207
  13.7 1.4 %collective-permute-start.6 = (bf16[32,2176]{1,0:T(8,128)(2,1)S(1)}, bf16[32,2176]{1,0:T(8,128)(2,1)S(1)}, u32[]{:S(2)}, u32[]{:S(2)}) collective-permute-start(bf16[32,2176]{1,0:T(8,128)(2,1)S(1)} %collective-permute-done.2.refs_1_), channel_id=1, source_target_pairs={{0,2},{2,0},{4,6},{6,4},{8,10},{10,8},{12,14},{14,12},{16,18},{18,... | collective-permute-start | bytes 417800 | tf_op jit(solution)/shard_map/ppermute | solution.py:207
  14.7 1.4 %collective-permute-start.5 = (bf16[32,2176]{1,0:T(8,128)(2,1)S(1)}, bf16[32,2176]{1,0:T(8,128)(2,1)S(1)}, u32[]{:S(2)}, u32[]{:S(2)}) collective-permute-start(bf16[32,2176]{1,0:T(8,128)(2,1)S(1)} %broadcast_select_fusion), channel_id=1, source_target_pairs={{0,2},{2,0},{4,6},{6,4},{8,10},{10,8},{12,14},{14,12},{16,18},{18,... | collective-permute-start | bytes 417800 | tf_op jit(solution)/shard_map/ppermute | solution.py:207
